TPU v7x, 32 devices: a whole 2x2x4 slice. The times are simulated.
32 devices in a mesh: seq: 8 (over z, y), head: 4 (over x, core).
Axes of the slice: x: 2, y: 2, z: 4, core: 2. Of those that a mesh axis runs over, the one named last changes fastest.
Arguments:
- query_rows: bfloat16 [2, 2048, 1024], P(None, 'seq', 'head'), may hold values from -70 to 70
- key_rows: bfloat16 [2, 2048, 1024], P(None, 'seq', 'head'), may hold values from -4.5 to 4.5
- value_rows: bfloat16 [2, 2048, 1024], P(None, 'seq', 'head'), may hold values from -6 to 6
- first_fast: float32 [4, 256, 512], P('head'), may hold values from -0.375 to 0.375
- third_fast: float32 [4, 256, 512], P('head'), may hold values from -0.375 to 0.375
- second_fast: float32 [4, 512, 256], P('head'), may hold values from -0.25 to 0.25
- out_proj: bfloat16 [1024, 1024], P('head'), may hold values from -0.1875 to 0.1875
- teacher: bfloat16 [2, 2048, 1024], P(None, 'seq'), may hold values from -31 to 31
Outputs:
- student: bfloat16 [2, 2048, 1024], P(None, 'seq', 'head')
- out_grad: float32 [1024, 1024], P('head')
- new_first: float32 [4, 256, 512], P('head')
- new_third: float32 [4, 256, 512], P('head')
- new_second: float32 [4, 512, 256], P('head')
- distill_loss: float32 [], replicated
All inputs are finite; a program needn't handle non-finite values.
Results may differ from a plain program's by a relative error of at most 0.012.
Values may be sent and summed in bfloat16 or wider, within the bound.
No kernel may reach another device: no remote copies, remote signals or barrier semaphores. Data moves between devices by JAX's collectives and lax.ppermute only.
A program may use at most 64 MiB of HBM per device.

v0:
```python
import math

import jax
import jax.numpy as jnp
from jax import lax
from jax.sharding import PartitionSpec as P

WINDOW = 256
NS_STEPS = 5


PRECISE = lax.Precision.HIGHEST
SCHULZ_COEFFS = (3.4445, -4.775, 2.0315)
LEARN_RATE = 0.5
EPSILON = 1e-06


def from_behind(block, axis, distance):
    devices = range(lax.axis_size(axis))
    route = [((i - distance) % len(devices), i) for i in devices]
    return lax.ppermute(block, axis, route)


def orthogonalize(matrix):
    current = matrix / (jnp.sqrt(jnp.sum(matrix * matrix)) + EPSILON)
    for sweep in range(NS_STEPS):
        gram_mat = jnp.dot(current, current.T, precision=PRECISE)
        poly_mat = SCHULZ_COEFFS[1] * gram_mat + SCHULZ_COEFFS[2] * jnp.dot(
            gram_mat, gram_mat, precision=PRECISE
        )
        current = SCHULZ_COEFFS[0] * current + jnp.dot(poly_mat, current, precision=PRECISE)
    return current


def fast_forward(w_one, w_three, w_two, inputs):
    gate_act = jnp.dot(inputs, w_one, precision=PRECISE)
    up_act = jnp.dot(inputs, w_three, precision=PRECISE)
    hidden = jax.nn.silu(gate_act) * up_act
    return (jnp.dot(hidden, w_two, precision=PRECISE), gate_act, up_act, hidden)


def fast_gradients(w_one, w_three, w_two, inputs, targets):
    unused, gate_act, up_act, hidden = fast_forward(w_one, w_three, w_two, inputs)
    grad_two = -jnp.dot(hidden.T, targets, precision=PRECISE)
    d_hidden = -jnp.dot(targets, w_two.T, precision=PRECISE)
    sigmoid_gate = jax.nn.sigmoid(gate_act)
    d_gate = d_hidden * up_act * sigmoid_gate * (1.0 + gate_act * (1.0 - sigmoid_gate))
    d_up = d_hidden * gate_act * sigmoid_gate
    grad_one = jnp.dot(inputs.T, d_gate, precision=PRECISE)
    grad_three = jnp.dot(inputs.T, d_up, precision=PRECISE)
    return (grad_one, grad_three, grad_two)


def rms_scale(values):
    return values * lax.rsqrt(jnp.mean(values * values, axis=-1, keepdims=True) + EPSILON)


def realign(piece, seq_pos):
    moved = jnp.concatenate([jnp.zeros_like(piece[:1]), piece[:-1]], axis=0)
    return jnp.where(seq_pos == 0, moved, piece)


def head_mix(mixed, projection, teacher_block):
    col_width = teacher_block.shape[2] // lax.axis_size("head")
    col_start = lax.axis_index("head") * col_width
    wide_mixed = lax.all_gather(mixed, "head", axis=2, tiled=True)
    own_sum = jnp.einsum("ctd,de->cte", wide_mixed, projection, preferred_element_type=jnp.float32)
    own_teacher = lax.dynamic_slice_in_dim(teacher_block, col_start, col_width, 2)
    own_diff = own_sum - own_teacher.astype(jnp.float32)
    resid = lax.all_gather(own_diff.astype(jnp.bfloat16), "head", axis=2, tiled=True)
    term = jnp.einsum("ctd,cte->de", mixed, resid, preferred_element_type=jnp.float32)
    return (own_sum.astype(jnp.bfloat16), term, jnp.sum(own_diff * own_diff))


def local(query_rows, key_rows, value_rows, first_fast, third_fast, second_fast, out_proj, teacher):
    block_count, tok_dev, head_dim = query_rows.shape
    projection = lax.all_to_all(out_proj, "head", split_axis=1, concat_axis=0, tiled=True)
    seq_pos = lax.axis_index("seq")
    block_len = tok_dev * lax.axis_size("seq")
    rim_keys, rim_values = from_behind((key_rows, value_rows), "seq", 1)
    keys_all = jnp.concatenate([realign(rim_keys, seq_pos), key_rows], axis=1)
    values_all = jnp.concatenate([realign(rim_values, seq_pos), value_rows], axis=1)
    block_base = jnp.arange(block_count, dtype=jnp.int32)[:, None] * block_len + seq_pos * tok_dev
    query_pos = block_base + jnp.arange(tok_dev, dtype=jnp.int32)[None, :]
    key_pos = block_base - WINDOW + jnp.arange(WINDOW + tok_dev, dtype=jnp.int32)[None, :]
    scores = jnp.einsum(
        "cqd,ckd->cqk", query_rows, keys_all, preferred_element_type=jnp.float32
    ) * (1.0 / math.sqrt(head_dim))
    spacing = query_pos[:, :, None] - key_pos[:, None, :]
    allowed = (spacing >= 0) & (spacing < WINDOW) & (key_pos[:, None, :] >= 0)
    masked = jnp.where(allowed, scores, -1e30)
    top_score = jnp.max(masked, axis=2, keepdims=True)
    expd = jnp.where(allowed, jnp.exp(masked - top_score), 0.0)
    weights = (expd / jnp.sum(expd, axis=2, keepdims=True)).astype(jnp.bfloat16)
    attention = jnp.einsum("cqk,ckd->cqd", weights, values_all, preferred_element_type=jnp.float32)
    w_one, w_three, w_two = (first_fast[0], third_fast[0], second_fast[0])
    mixed_blocks = []
    for block_idx in range(block_count):
        q_float = query_rows[block_idx].astype(jnp.float32)
        k_float = key_rows[block_idx].astype(jnp.float32)
        v_float = value_rows[block_idx].astype(jnp.float32)
        fast_out = fast_forward(w_one, w_three, w_two, q_float)[0]
        mixed_now = (attention[block_idx] + rms_scale(fast_out)).astype(jnp.bfloat16)
        grad_one, grad_three, grad_two = fast_gradients(w_one, w_three, w_two, k_float, v_float)
        mixed_blocks.append(mixed_now)
        grad_one, grad_three, grad_two = lax.psum((grad_one, grad_three, grad_two), "seq")
        w_one = w_one - LEARN_RATE * orthogonalize(grad_one)
        w_three = w_three - LEARN_RATE * orthogonalize(grad_three)
        w_two = w_two - LEARN_RATE * orthogonalize(grad_two.T).T
    student, term, loss_part = head_mix(jnp.stack(mixed_blocks), projection, teacher)
    out_total = lax.psum(term, "seq")
    total_rows = block_count * block_len
    out_grad = out_total / math.sqrt(total_rows)
    distill_loss = lax.psum(loss_part, ("seq", "head")) / (total_rows * out_proj.shape[1])
    return (student, out_grad, w_one[None], w_three[None], w_two[None], distill_loss)


def solution(mesh):
    in_specs = (
        P(None, "seq", "head"),
        P(None, "seq", "head"),
        P(None, "seq", "head"),
        P("head", None, None),
        P("head", None, None),
        P("head", None, None),
        P("head", None),
        P(None, "seq", None),
    )
    out_specs = (
        P(None, "seq", "head"),
        P("head", None),
        P("head", None, None),
        P("head", None, None),
        P("head", None, None),
        P(),
    )
    return jax.shard_map(local, mesh=mesh, in_specs=in_specs, out_specs=out_specs, check_vma=False)
```

profile of v0, /device:TPU:0, one launch (start us, length us, event | category | flops | bytes accessed | tf_op | source)
XLA Modules:
  0.0 362.9 jit_solution(10785341162138251714)
XLA Ops:
  7.2 3.0 collective-permute-start.1
  10.3 1.5 collective-permute-start
  11.8 1.6 convolution_negate_fusion.3
  14.8 1.4 convolution_bitcast_fusion.6
  16.3 1.5 convolution_bitcast_fusion.8
  17.8 1.5 convolution_negate_fusion.2
  26.4 2.1 fusion.190
  28.5 2.4 fusion.58
  30.9 78.6 %all-reduce.9.cloned.1.call-done = (f32[256,512]{0,1:T(8,128)}, f32[256,512]{0,1:T(8,128)}, f32[512,256]{1,0:T(8,128)}) async-done(((f32[256,512]{0,1:T(8,128)}, f32[256,512]{0,1:T(8,128)}, f32[512,256]{1,0:T(8,128)}), (f32[256,512]{0,1:T(8,128)}, f32[256,512]{0,1:T(8,128)}, f32[512,256]{1,0:T(8,128)})) %all-reduce.9.cloned.1.call-update) | async-done | bytes 1572880 | tf_op jit(solution)/shard_map/psum | solution.py:106
  109.4 2.0 multiply_reduce_fusion.5
  125.2 1.4 fusion.193
  153.6 3.5 all-to-all-start
  157.2 13.6 %all-to-all-done = bf16[256,4,256]{2,0,1:T(8,128)(2,1)S(1)} async-done(((bf16[256,4,256]{2,0,1:T(8,128)(2,1)}), bf16[256,4,256]{2,0,1:T(8,128)(2,1)S(1)}, u32[]{:S(2)}, u32[]{:S(2)}) %all-to-all-start) | async-done | bytes 524320 | tf_op jit(solution)/shard_map/all_to_all | solution.py:77
  170.8 2.3 all-gather.3.cloned.1.call-done
  173.2 3.1 multiply_reduce_fusion
  178.1 1.4 convolution_bitcast_fusion.1
  179.6 1.4 convolution_negate_fusion
  181.0 1.5 convolution_bitcast_fusion.2
  182.5 9.3 %all-gather.5.cloned.1.call-done = bf16[2,256,1024]{2,1,0:T(8,128)(2,1)} async-done(((bf16[2,256,256]{2,1,0:T(8,128)(2,1)}), bf16[2,256,1024]{2,1,0:T(8,128)(2,1)}) %all-gather.5.cloned.1.call-update) | async-done | bytes 1048592 | tf_op jit(solution)/shard_map/all_gather | solution.py:70
  191.8 2.7 convolution_bitcast_fusion
  194.5 43.4 %psum.63 = f32[]{:T(128)} all-reduce(f32[]{:T(128)} %get-tuple-element.19), channel_id=1, replica_groups=mesh['seq'=8,'head'=4] {'seq','head'}, use_global_device_ids=true, to_apply=%region_18.19 | all-reduce | flops 1 | bytes 8 | tf_op jit(solution)/shard_map/psum | solution.py:114
  238.5 75.7 %all-reduce.7.cloned.1.call-done = (f32[256,1024]{1,0:T(8,128)}, f32[256,512]{0,1:T(8,128)}, f32[256,512]{0,1:T(8,128)}, f32[512,256]{1,0:T(8,128)}) async-done(((f32[256,1024]{1,0:T(8,128)}, f32[256,512]{0,1:T(8,128)}, f32[256,512]{0,1:T(8,128)}, f32[512,256]{1,0:T(8,128)}), (f32[256,1024]{1,0:T(8,128)}, f32[256,512]{0,1:T(8,128)}, f32[256,512]{0,1:T(8,128)}, ...) | async-done | bytes 2621456 | tf_op jit(solution)/shard_map/psum | solution.py:111
  314.2 2.4 broadcast_multiply_fusion
  353.5 1.5 fusion.10
  (176 shorter events, 83.1 us)
Async XLA Ops:
  7.2 6.2 %copy-start.5 = (bf16[2,256,256]{2,1,0:T(8,128)(2,1)S(1)}, bf16[2,256,256]{2,1,0:T(8,128)(2,1)}, u32[]{:S(2)}) copy-start(bf16[2,256,256]{2,1,0:T(8,128)(2,1)} %param.9) | copy-start | bytes 786436
  7.2 6.2 %copy-start.1 = (f32[1,256,512]{2,1,0:T(8,128)S(1)}, f32[1,256,512]{2,1,0:T(8,128)}, u32[]{:S(2)}) copy-start(f32[1,256,512]{2,1,0:T(8,128)} %param.11) | copy-start | bytes 1572868
  7.2 102.3 %all-reduce.9.cloned.1.call-start = ((), (), s32[]{:S(2)}) async-start(), calls=%async_computation.4 | async-start | bytes 3145728 | tf_op jit(solution)/shard_map/psum | solution.py:106
  7.2 16.8 %collective-permute-start.1 = (bf16[2,256,256]{2,1,0:T(8,128)(2,1)}, bf16[2,256,256]{2,1,0:T(8,128)(2,1)S(1)}, u32[]{:S(2)}, u32[]{:S(2)}) collective-permute-start(bf16[2,256,256]{2,1,0:T(8,128)(2,1)} %param.10), channel_id=1, source_target_pairs={{28,0},{0,4},{4,8},{8,12},{12,16},{16,20},{20,24},{24,28},{29,1},{... | collective-permute-start | bytes 786440 | tf_op jit(solution)/shard_map/ppermute | solution.py:21
  10.3 15.2 %collective-permute-start = (bf16[2,256,256]{2,1,0:T(8,128)(2,1)}, bf16[2,256,256]{2,1,0:T(8,128)(2,1)S(1)}, u32[]{:S(2)}, u32[]{:S(2)}) collective-permute-start(bf16[2,256,256]{2,1,0:T(8,128)(2,1)} %param.9), channel_id=1, source_target_pairs={{28,0},{0,4},{4,8},{8,12},{12,16},{16,20},{20,24},{24,28},{29,1},{... | collective-permute-start | bytes 786440 | tf_op jit(solution)/shard_map/ppermute | solution.py:21
  13.4 1.0 copy-start.4
  16.3 1.5 copy-start.19
  19.3 153.9 %all-gather.3.cloned.1.call-start = ((), (), s32[]{:S(2)}) async-start(), calls=%async_computation.1 | async-start | bytes 1310720 | tf_op jit(solution)/shard_map/all_gather | solution.py:66
  20.7 1.0 copy-start
  26.4 2.1 copy-start.20
  109.4 2.7 copy-start.11
  121.4 1.8 copy-start.10
  134.2 1.2 copy-start.2
  147.2 1.0 copy-start.15
  147.2 1.1 copy-start.18
  149.5 1.2 copy-start.9
  150.6 1.0 copy-start.7
  151.7 1.1 copy-start.14
  153.6 17.2 %all-to-all-start = ((bf16[256,4,256]{2,0,1:T(8,128)(2,1)}), bf16[256,4,256]{2,0,1:T(8,128)(2,1)S(1)}, u32[]{:S(2)}, u32[]{:S(2)}) async-start(bf16[256,4,256]{2,0,1:T(8,128)(2,1)} %bitcast.348), calls=%async_computation | async-start | bytes 1048576 | tf_op jit(solution)/shard_map/all_to_all | solution.py:77
  157.1 34.6 %all-gather.5.cloned.1.call-start = ((), (), s32[]{:S(2)}) async-start(), calls=%async_computation.2 | async-start | bytes 1310720 | tf_op jit(solution)/shard_map/all_gather | solution.py:70
  176.3 137.9 %all-reduce.7.cloned.1.call-start = ((), (), s32[]{:S(2)}) async-start(), calls=%async_computation.3 | async-start | bytes 5242880 | tf_op jit(solution)/shard_map/psum | solution.py:111
  314.2 2.4 copy-start.13
  328.3 1.0 copy-start.12
  341.2 1.0 copy-start.3
  (6 other events, 5.4 us)
Sparse Core Ops, SparseCore 0:
  19.4 89.9 all-reduce.8
  152.6 20.5 all-gather.2
  176.4 15.3 all-gather.4
  196.2 117.9 all-reduce.6
where the time goes:
time: 369 us; the launch traced here: 363 us
  waiting for transfers between devices  180 us (49%)
  matrix products  91 us (25%)
  blocking collectives  43.4 us (12%)
  between operations  21 us (6%)
  local copies, waits for them, and re-layouts  10.7 us (3%)
  other arithmetic  8.44 us (2%)
  starting transfers between devices  8.17 us (2%)
    psum x1, waiting for transfers between devices, local(): lax.psum((grad_one, grad_three, grad_two), 'seq')  78.6 us
    psum x1, waiting for transfers between devices, local(): out_total = lax.psum(term, 'seq')  75.7 us
    psum x1, blocking collectives, local(): lax.psum(loss_part, ('seq', 'head')) / (total_rows * out_proj.shape[1])  43.4 us
    dot_general x30, matrix products, orthogonalize(): gram_mat = jnp.dot(current, current.T, precision=PRECISE)  31.5 us
    dot_general x30, matrix products, orthogonalize(): jnp.dot(poly_mat, current, precision=PRECISE)  20 us
    all_to_all x1, waiting for transfers between devices, local(): lax.all_to_all(out_proj, 'head', split_axis=1, concat_axis=0, tiled=True)  13.6 us
    dot_general x30, matrix products, orthogonalize(): jnp.dot(gram_mat, gram_mat, precision=PRECISE)  12.1 us
    all_gather x1, waiting for transfers between devices, head_mix(): lax.all_gather(own_diff.astype(jnp.bfloat16), 'head', axis=2, tiled=True)  9.25 us
  transfers between devices with their start and end apart: 7, of which 6 were waited for; matrix products, arithmetic and copies ran while one was open for 6% of the time, Pallas kernels for 0%

commit v1 on v0

v1 whole, which is shorter than its diff:
```python
import functools
import math

import jax
import jax.numpy as jnp
from jax import lax
from jax.experimental import pallas as pl
from jax.experimental.pallas import tpu as pltpu
from jax.sharding import PartitionSpec as P

WINDOW = 256
NS_STEPS = 5
SCHULZ_COEFFS = (3.4445, -4.775, 2.0315)
LEARN_RATE = 0.5
EPSILON = 1e-06
LANES = 128
LOSS_ROWS = 16
VMEM_BYTES = 40 * 1024 * 1024

F32 = jnp.float32
BF16 = jnp.bfloat16


def mm(a, b):
    return jnp.dot(a, b, preferred_element_type=F32)


def mm_nt(a, b):
    return lax.dot_general(a, b, (((1,), (1,)), ((), ())), preferred_element_type=F32)


def mm_tn(a, b):
    return lax.dot_general(a, b, (((0,), (0,)), ((), ())), preferred_element_type=F32)


def split(x):
    high = x.astype(BF16)
    return high, (x - high.astype(F32)).astype(BF16)


def token_gradients(weights, keys, values):
    w_one, w_three, w_two_t = weights
    gate = mm(keys, w_one)
    up = mm(keys, w_three)
    d_hidden = -mm(values, w_two_t)
    sig = jax.nn.sigmoid(gate)
    silu = gate * sig
    d_gate = d_hidden * up * sig * (1.0 + gate * (1.0 - sig))
    d_up = d_hidden * silu
    hidden = silu * up
    return (
        mm_tn(keys, d_gate.astype(BF16)),
        mm_tn(keys, d_up.astype(BF16)),
        -mm_tn(values, hidden.astype(BF16)),
    )


def orthogonalize(mats):
    a, b, c = SCHULZ_COEFFS
    centre = -b / (2.0 * c)
    rest = a - b * b / (4.0 * c)
    rows = mats[0].shape[0]
    shape = (rows, rows)
    diag = lax.broadcasted_iota(jnp.int32, shape, 0) == lax.broadcasted_iota(jnp.int32, shape, 1)
    xs = [m * (1.0 / (jnp.sqrt(jnp.sum(m * m)) + EPSILON)) for m in mats]
    for sweep in range(NS_STEPS):
        if sweep < 2:
            lows = [x.astype(BF16) for x in xs]
            grams = [mm_nt(x, x) for x in lows]
            halves = [g.astype(BF16) for g in grams]
            polys = [(b * g + c * mm(h, h)).astype(BF16) for g, h in zip(grams, halves)]
            xs = [a * x + mm(p, low) for x, p, low in zip(xs, polys, lows)]
        elif sweep == 2:
            pairs = [split(x) for x in xs]
            grams = [mm_nt(h, h) + mm_nt(h, l) + mm_nt(l, h) for h, l in pairs]
            gpairs = [split(g) for g in grams]
            polys = [
                b * g + c * (mm(h, h) + mm(h, l) + mm(l, h)) for g, (h, l) in zip(grams, gpairs)
            ]
            ppairs = [split(p) for p in polys]
            xs = [
                a * x + (mm(ph, h) + mm(ph, l) + mm(pl_, h))
                for x, (ph, pl_), (h, l) in zip(xs, ppairs, pairs)
            ]
        else:
            lows = [x.astype(BF16) for x in xs]
            grams = [mm_nt(x, x) for x in lows]
            moved = [jnp.where(diag, g - centre, g).astype(BF16) for g in grams]
            polys = [(c * mm(h, h)).astype(BF16) for h in moved]
            xs = [rest * x + mm(p, low) for x, p, low in zip(xs, polys, lows)]
    return xs


def normed_forward(weights, queries):
    w_one, w_three, w_two_t = [split(w) for w in weights]
    gate = mm(queries, w_one[0]) + mm(queries, w_one[1])
    up = mm(queries, w_three[0]) + mm(queries, w_three[1])
    hidden = (gate * jax.nn.sigmoid(gate) * up).astype(BF16)
    out = mm_nt(hidden, w_two_t[0]) + mm_nt(hidden, w_two_t[1])
    return out * lax.rsqrt(jnp.mean(out * out, axis=-1, keepdims=True) + EPSILON)


def window_attention(queries, own, behind, has_behind):
    tok, width = queries.shape
    head_dim = width
    scale = 1.0 / math.sqrt(head_dim)
    shape = (tok, tok)
    row = lax.broadcasted_iota(jnp.int32, shape, 0)
    col = lax.broadcasted_iota(jnp.int32, shape, 1)
    allow_own = (row >= col) & (row - col < WINDOW)
    allow_behind = (row + tok - col < WINDOW) & has_behind
    s_own = jnp.where(allow_own, mm_nt(queries, own[:, :width]) * scale, -1e30)
    s_behind = jnp.where(allow_behind, mm_nt(queries, behind[:, :width]) * scale, -1e30)
    top = jnp.maximum(
        jnp.max(s_own, axis=1, keepdims=True), jnp.max(s_behind, axis=1, keepdims=True)
    )
    e_own = jnp.where(allow_own, jnp.exp(s_own - top), 0.0)
    e_behind = jnp.where(allow_behind, jnp.exp(s_behind - top), 0.0)
    total = jnp.sum(e_own, axis=1, keepdims=True) + jnp.sum(e_behind, axis=1, keepdims=True)
    inv = 1.0 / total
    return mm((e_own * inv).astype(BF16), own[:, width:]) + mm(
        (e_behind * inv).astype(BF16), behind[:, width:]
    )


def call(kernel, outs, args, flops=0, scratch=()):
    vmem = pl.BlockSpec(memory_space=pltpu.VMEM)
    size = sum(math.prod(a.shape) * a.dtype.itemsize for a in list(args) + list(outs))
    return pl.pallas_call(
        kernel,
        out_shape=tuple(jax.ShapeDtypeStruct(o.shape, o.dtype) for o in outs),
        in_specs=[vmem] * len(args),
        out_specs=tuple([vmem] * len(outs)),
        scratch_shapes=list(scratch),
        compiler_params=pltpu.CompilerParams(vmem_limit_bytes=VMEM_BYTES),
        cost_estimate=pl.CostEstimate(flops=flops, bytes_accessed=size, transcendentals=0),
    )(*args)


def like(shape, dtype):
    return jax.ShapeDtypeStruct(shape, dtype)


def gradients(weights, runs, before):
    rows, hidden = weights[0].shape
    count = len(runs)

    def kernel(*refs):
        w = [r[...].astype(BF16) for r in refs[:3]]
        run_refs = refs[3 : 3 + count]
        prev = refs[3 + count : -3]
        sums = [p[...] for p in prev] if prev else None
        for run in run_refs:
            new = token_gradients(w, run[:, :rows], run[:, rows:])
            sums = list(new) if sums is None else [s + n for s, n in zip(sums, new)]
        for out, value in zip(refs[-3:], sums):
            out[...] = value

    tokens = sum(r.shape[0] for r in runs)
    args = list(weights) + list(runs) + (list(before) if before is not None else [])
    outs = [like((rows, hidden), F32)] * 3
    return call(kernel, outs, args, flops=12 * tokens * rows * hidden)


def update(weights, grads, last_runs, queries=None, attention=None, block=None):
    rows, hidden = weights[0].shape
    count = len(last_runs)
    mixes = queries is not None

    def kernel(*refs):
        w = [r[...] for r in refs[:3]]
        sums = [r[...] for r in refs[3:6]]
        run_refs = refs[6 : 6 + count]
        low = [x.astype(BF16) for x in w]
        for run in run_refs:
            new = token_gradients(low, run[:, :rows], run[:, rows:])
            sums = [s + n for s, n in zip(sums, new)]
        ortho = orthogonalize(sums)
        fresh = [x - LEARN_RATE * o for x, o in zip(w, ortho)]
        if mixes:
            q_ref, att_ref = refs[6 + count : 8 + count]
            outs = refs[8 + count :]
            for out, value in zip(outs, fresh):
                out[...] = value
            outs[3][...] = (att_ref[...] + normed_forward(fresh, q_ref[block])).astype(BF16)
        else:
            outs = refs[6 + count :]
            outs[0][0] = fresh[0]
            outs[1][0] = fresh[1]
            outs[2][0] = fresh[2].T

    args = list(weights) + list(grads) + list(last_runs)
    if mixes:
        args += [queries, attention]
        outs = [like((rows, hidden), F32)] * 3 + [like(queries.shape[1:], BF16)]
    else:
        outs = [like((1, rows, hidden), F32)] * 2 + [like((1, hidden, rows), F32)]
    flops = 3 * 5 * 2 * (2 * rows * rows * hidden + rows**3) * 2
    return call(kernel, outs, args, flops=flops)


def attend(queries, own, behind, block):
    def kernel(q_ref, own_ref, behind_ref, out_ref):
        has_behind = (lax.axis_index("seq") > 0) | (block > 0)
        out_ref[...] = window_attention(q_ref[block], own_ref[...], behind_ref[...], has_behind)

    tok, width = queries.shape[1:]
    return call(
        kernel, [like((tok, width), F32)], [queries, own, behind], flops=8 * tok * tok * width
    )[0]


def first_mix(queries, own, behind, weights):
    def kernel(q_ref, own_ref, behind_ref, one_ref, three_ref, two_ref, out_ref):
        has_behind = lax.axis_index("seq") > 0
        queries = q_ref[0]
        att = window_attention(queries, own_ref[...], behind_ref[...], has_behind)
        w = [one_ref[...], three_ref[...], two_ref[...]]
        out_ref[...] = (att + normed_forward(w, queries)).astype(BF16)

    tok, width = queries.shape[1:]
    return call(
        kernel,
        [like((tok, width), BF16)],
        [queries, own, behind] + list(weights),
        flops=20 * tok * tok * width,
    )[0]


def project(mixed_parts, proj_parts, teacher, block, students):
    count = len(mixed_parts)
    tok, width = mixed_parts[0].shape
    cols = teacher.shape[2]

    def kernel(*refs):
        mixed_refs, proj_refs = refs[:count], refs[count : 2 * count]
        teacher_ref = refs[2 * count]
        student_ref, resid_ref, loss_ref, low_ref = refs[2 * count + 1 :]
        summed = mm(mixed_refs[0][...], proj_refs[0][...])
        for m, p in zip(mixed_refs[1:], proj_refs[1:]):
            summed = summed + mm(m[...], p[...])
        low_ref[...] = summed.astype(BF16)
        start = pl.multiple_of(lax.axis_index("head") * width, width)
        student_ref[...] = low_ref[:, pl.ds(start, width)]
        diff = summed - teacher_ref[block].astype(F32)
        resid_ref[...] = diff.astype(BF16)
        loss_ref[...] = jnp.full((8, LANES), jnp.sum(diff * diff), F32)

    return call(
        kernel,
        [like((tok, width), BF16), like((tok, cols), BF16), like((8, LANES), F32)],
        list(mixed_parts) + list(proj_parts) + [teacher],
        flops=2 * tok * cols * width * count,
        scratch=[pltpu.VMEM((tok, cols), BF16)],
    )


def loss_tile(loss):
    high = loss.astype(BF16).astype(F32)
    row = lax.broadcasted_iota(jnp.int32, (LOSS_ROWS, LANES), 0)
    return jnp.where(row < LOSS_ROWS // 2, high, loss - high).astype(BF16)


def tile_loss(tile):
    return jnp.sum(tile.astype(F32)) * (1.0 / (LOSS_ROWS // 2 * LANES))


def outer_halves(mixed, resids, losses):
    count = len(mixed)
    width = mixed[0].shape[1]
    cols = resids[0].shape[1]
    half = cols // 2

    def kernel(*refs):
        mixed_refs, resid_refs = refs[:count], refs[count : 2 * count]
        loss_refs = refs[2 * count : 3 * count]
        keep_ref, send_ref, loss_ref = refs[3 * count :]
        mine = lax.rem(lax.axis_index("seq"), 2)
        keep_at = pl.multiple_of(mine * half, half)
        send_at = pl.multiple_of((1 - mine) * half, half)
        keep = send = None
        for m, r in zip(mixed_refs, resid_refs):
            one = mm_tn(m[...], r[:, pl.ds(send_at, half)])
            two = mm_tn(m[...], r[:, pl.ds(keep_at, half)])
            send = one if send is None else send + one
            keep = two if keep is None else keep + two
        keep_ref[...] = keep
        send_ref[:width, :] = send.astype(BF16)
        loss = sum(jnp.max(r[...]) for r in loss_refs)
        loss_ref[...] = jnp.full((8, LANES), loss, F32)
        tile = loss_tile(loss)
        for at in range(0, half, LANES):
            send_ref[width:, at : at + LANES] = tile

    return call(
        kernel,
        [like((width, half), F32), like((width + LOSS_ROWS, half), BF16), like((8, LANES), F32)],
        list(mixed) + list(resids) + list(losses),
        flops=2 * count * mixed[0].shape[0] * width * cols,
    )


def outer_chunks(keep, got, loss, line):
    width, half = keep.shape
    chunk = half // line

    def kernel(keep_ref, got_ref, loss_ref, own_ref, new_loss_ref, *rest):
        sends, full_ref = rest[:-1], rest[-1]
        place = lax.div(lax.axis_index("seq"), 2)
        full_ref[...] = keep_ref[...] + got_ref[:width, :].astype(F32)
        total = jnp.max(loss_ref[...]) + tile_loss(got_ref[width:, :LANES])
        new_loss_ref[...] = jnp.full((8, LANES), total, F32)
        tile = loss_tile(total)

        def part(index):
            return full_ref[:, pl.ds(pl.multiple_of(index * chunk, chunk), chunk)]

        own_ref[...] = part(place)
        for offset, send in enumerate(sends, start=1):
            send[:width, :] = part(place ^ offset).astype(BF16)
            for at in range(0, chunk, LANES):
                send[width:, at : at + LANES] = tile

    message = like((width + LOSS_ROWS, chunk), BF16)
    return call(
        kernel,
        [like((width, chunk), F32), like((8, LANES), F32)] + [message] * (line - 1),
        [keep, got, loss],
        scratch=[pltpu.VMEM((width, half), F32)],
    )


def outer_total(own, loss, gots, grad_scale, loss_scale):
    width, chunk = own.shape

    def kernel(own_ref, loss_ref, *rest):
        got_refs, out_ref, new_loss_ref = rest[:-2], rest[-2], rest[-1]
        total = own_ref[...]
        sq = jnp.max(loss_ref[...])
        for got in got_refs:
            total = total + got[:width, :].astype(F32)
            sq = sq + tile_loss(got[width:, :LANES])
        out_ref[...] = (total * grad_scale).astype(BF16)
        new_loss_ref[...] = jnp.full((8, LANES), sq * loss_scale, F32)

    return call(
        kernel, [like((width, chunk), BF16), like((8, LANES), F32)], [own, loss] + list(gots)
    )


def assemble(pieces, places, cols):
    width, chunk = pieces[0].shape
    count = len(pieces)

    def kernel(*refs):
        out_ref = refs[-1]
        me = lax.axis_index("seq")
        for ref, table in zip(refs[:count], places):
            index = sum(jnp.where(me == d, c, 0) for d, c in enumerate(table))
            out_ref[:, pl.ds(pl.multiple_of(index * chunk, chunk), chunk)] = ref[...].astype(F32)

    return call(kernel, [like((width, cols), F32)], list(pieces))[0]


def ring_order(size):
    return list(range(0, size, 2)) + list(range(size - 1 - size % 2, 0, -2))


def ring_steps(block, axis, split_last):
    size = lax.axis_size(axis)
    order = ring_order(size)
    ahead = [(order[i], order[(i + 1) % size]) for i in range(size)]
    back = [(b, a) for a, b in ahead]

    def source(distance):
        table = [0] * size
        for i, d in enumerate(order):
            table[d] = order[(i - distance) % size]
        return table

    steps = []
    up = down = block
    for step in range(1, size // 2 + 1):
        if 2 * step == size:
            if split_last:
                rows = block.shape[0] // 2
                steps.append(
                    [
                        (lax.ppermute(up[:rows], axis, ahead), source(step)),
                        (lax.ppermute(down[rows:], axis, back), source(step)),
                    ]
                )
            else:
                steps.append([(lax.ppermute(up, axis, ahead), source(step))])
        else:
            up = lax.ppermute(up, axis, ahead)
            down = lax.ppermute(down, axis, back)
            steps.append([(up, source(step)), (down, source(-step))])
    return steps


def partner(block, axis, bit):
    size = lax.axis_size(axis)
    return lax.ppermute(block, axis, [(i ^ bit, i) for i in range(size)])


def cube_gather(block, axis):
    parts = [block]
    bit = lax.axis_size(axis) // 2
    while bit:
        parts += [partner(p, axis, bit) for p in parts]
        bit //= 2
    return parts


def from_behind(block, axis):
    size = lax.axis_size(axis)
    return lax.ppermute(block, axis, [((i - 1) % size, i) for i in range(size)])


def local(query_rows, key_rows, value_rows, first_fast, third_fast, second_fast, out_proj, teacher):
    block_count, tok, head_dim = query_rows.shape
    seq = lax.axis_size("seq")
    cols = out_proj.shape[1]
    total_rows = block_count * tok * seq
    last = seq - 1
    pos = lax.axis_index("seq")
    gathers = seq <= 8
    kv = [jnp.concatenate([key_rows[c], value_rows[c]], axis=1) for c in range(block_count)]
    weights = (first_fast[0], third_fast[0], second_fast[0].T)

    proj_parts = cube_gather(out_proj, "head")
    behind = []
    for c in range(block_count):
        rim = kv[c] if c == 0 else jnp.where(pos == last, kv[c - 1], kv[c])
        behind.append(from_behind(rim, "seq"))

    students, resids, losses, mixed_rows = [], [], [], []
    mixed = first_mix(query_rows, kv[0], behind[0], weights)
    for c in range(block_count):
        mixed_rows.append(mixed)
        student, resid, loss = project(cube_gather(mixed, "head"), proj_parts, teacher, c, None)
        students.append(student)
        resids.append(resid)
        losses.append(loss)
        if gathers:
            steps = ring_steps(kv[c], "seq", True)
            runs = [[block for block, _ in step] for step in steps]
            grads = gradients(weights, [kv[c]] + (runs[0] if len(runs) > 1 else []), None)
            middle = [r for step in runs[1:-1] for r in step]
            if middle:
                grads = gradients(weights, middle, grads)
            final = runs[-1] if runs else []
        else:
            grads = lax.psum(gradients(weights, [kv[c]], None), "seq")
            final = []
        if c + 1 < block_count:
            attention = attend(query_rows, kv[c + 1], behind[c + 1], c + 1)
            *fresh, mixed = update(weights, grads, final, query_rows, attention, c + 1)
            weights = tuple(fresh)
        else:
            new_first, new_third, new_second = update(weights, grads, final)

    student = jnp.stack(students)
    grad_scale = 1.0 / math.sqrt(total_rows)
    loss_scale = 1.0 / (total_rows * cols)
    if seq >= 4 and seq & (seq - 1) == 0 and cols % (seq * LANES) == 0:
        line = seq // 2
        keep, send, loss = outer_halves(mixed_rows, resids, losses)
        own, loss, *sends = outer_chunks(keep, partner(send, "seq", 1), loss, line)
        gots = [partner(s, "seq", 2 * (m + 1)) for m, s in enumerate(sends)]
        piece, loss = outer_total(own, loss, gots, grad_scale, loss_scale)
        steps = ring_steps(piece, "seq", False)

        def place(d):
            return (d % 2) * line + d // 2

        pieces = [piece] + [p for step in steps for p, _ in step]
        tables = [list(range(seq))] + [t for step in steps for _, t in step]
        out_grad = assemble(pieces, [[place(d) for d in t] for t in tables], cols)
        distill_loss = loss[0, 0]
    else:
        term = sum(
            lax.dot_general(m, r, (((0,), (0,)), ((), ())), preferred_element_type=F32)
            for m, r in zip(mixed_rows, resids)
        )
        term, loss = lax.psum((term, sum(losses)), "seq")
        out_grad = term * grad_scale
        distill_loss = loss[0, 0] * loss_scale
    return (student, out_grad, new_first, new_third, new_second, distill_loss)


def solution(mesh):
    in_specs = (
        P(None, "seq", "head"),
        P(None, "seq", "head"),
        P(None, "seq", "head"),
        P("head", None, None),
        P("head", None, None),
        P("head", None, None),
        P("head", None),
        P(None, "seq", None),
    )
    out_specs = (
        P(None, "seq", "head"),
        P("head", None),
        P("head", None, None),
        P("head", None, None),
        P("head", None, None),
        P(),
    )
    return jax.shard_map(local, mesh=mesh, in_specs=in_specs, out_specs=out_specs, check_vma=False)
```

time: 369 us -> 113 us (0.31); the launches traced: 363 us -> 112 us
  waiting for transfers between devices: 180 us -> 34.1 us
  matrix products: 91 us -> 0 us
  blocking collectives: 43.4 us -> 0 us
  starting transfers between devices: 8.17 us -> 40.7 us
  Pallas kernels: 0 us -> 30.9 us
  between operations: 21 us -> 0.91 us
  other arithmetic: 8.44 us -> 1.52 us
  local copies, waits for them, and re-layouts: 10.7 us -> 4.35 us
    psum x2 -> x0, waiting for transfers between devices: 154 us -> none  [the longest x1 78.6 us: local(): lax.psum((grad_one, grad_three, grad_two), 'seq')]
    dot_general x111 -> x0, matrix products: 88.9 us -> none  [the longest x30 31.5 us: orthogonalize(): gram_mat = jnp.dot(current, current.T, precision=PRECISE)]
    psum x1 -> x0, blocking collectives: 43.4 us -> none  [local(): lax.psum(loss_part, ('seq', 'head')) / (total_rows * out_proj.shape[1])]
    ppermute x2 -> x38, starting transfers between devices: 4.54 us -> 40.7 us  [the longest x13 12.6 us: partner(): return lax.ppermute(block, axis, [(i ^ bit, i) for i in range(size)])]
    ppermute x2 -> x38, waiting for transfers between devices: 0.67 us -> 34.1 us  [the longest x13 12.8 us: partner(): return lax.ppermute(block, axis, [(i ^ bit, i) for i in range(size)])]
    pallas_call x0 -> x14, Pallas kernels: none -> 30.9 us  [call(): pl.pallas_call(kernel, out_shape=tuple((jax.ShapeDtypeStruct(o.shape, o.d...]
    all_to_all x1 -> x0, waiting for transfers between devices: 13.6 us -> none  [local(): lax.all_to_all(out_proj, 'head', split_axis=1, concat_axis=0, tiled=True)]
    all_gather x2 -> x0, waiting for transfers between devices: 11.6 us -> none  [the longest x1 9.25 us: head_mix(): lax.all_gather(own_diff.astype(jnp.bfloat16), 'head', axis=2, tiled=True)]
  transfers between devices with their start and end apart: 7 -> 38, of which waited for: 6 -> 11; matrix products, arithmetic and copies ran while one was open for 6% -> 2% of each run, Pallas kernels for 0% -> 26%
where the time goes in v1:
time: 113 us; the launch traced here: 112 us
  starting transfers between devices  40.7 us (36%)
  waiting for transfers between devices  34.1 us (30%)
  Pallas kernels  30.9 us (27%)
  local copies, waits for them, and re-layouts  4.35 us (4%)
  other arithmetic  1.52 us (1%)
    pallas_call x14, Pallas kernels, call(): pl.pallas_call(kernel, out_shape=tuple((jax.ShapeDtypeStruct(o.shape, o.d...  30.9 us
    ppermute x13, waiting for transfers between devices, partner(): return lax.ppermute(block, axis, [(i ^ bit, i) for i in range(size)])  12.8 us
    ppermute x13, starting transfers between devices, partner(): return lax.ppermute(block, axis, [(i ^ bit, i) for i in range(size)])  12.6 us
    ppermute x9, starting transfers between devices, ring_steps(): up = lax.ppermute(up, axis, ahead)  11.6 us
    ppermute x9, waiting for transfers between devices, ring_steps(): up = lax.ppermute(up, axis, ahead)  9.46 us
    ppermute x2, waiting for transfers between devices, from_behind(): return lax.ppermute(block, axis, [((i - 1) % size, i) for i in range(size)])  9.23 us
    ppermute x9, starting transfers between devices, ring_steps(): down = lax.ppermute(down, axis, back)  8.07 us
    ppermute x2, starting transfers between devices, from_behind(): return lax.ppermute(block, axis, [((i - 1) % size, i) for i in range(size)])  3.26 us
  transfers between devices with their start and end apart: 38, of which 11 were waited for; matrix products, arithmetic and copies ran while one was open for 2% of the time, Pallas kernels for 26%

profile of v1, /device:TPU:0, one launch (start us, length us, event | category | flops | bytes accessed | tf_op | source)
XLA Modules:
  0.0 112.5 jit_solution(11191521253600278978)
XLA Ops:
  2.6 3.0 %collective-permute-start.7 = (bf16[256,512]{1,0:T(8,128)(2,1)S(1)}, bf16[256,512]{1,0:T(8,128)(2,1)S(1)}, u32[]{:S(2)}, u32[]{:S(2)}) collective-permute-start(bf16[256,512]{1,0:T(8,128)(2,1)S(1)} %get-tuple-element.77.own_ref.refs_3_), channel_id=1, source_target_pairs={{0,8},{8,16},{16,24},{24,28},{28,20},{20,12},{12,4},{4,0},{1,9},{9... | collective-permute-start | bytes 786440 | tf_op jit(solution)/shard_map/ppermute | solution.py:396
  5.6 6.2 %collective-permute-done.7.refs_4_ = bf16[256,512]{1,0:T(8,128)(2,1)S(1)} collective-permute-done((bf16[256,512]{1,0:T(8,128)(2,1)S(1)}, bf16[256,512]{1,0:T(8,128)(2,1)S(1)}, u32[]{:S(2)}, u32[]{:S(2)}) %collective-permute-start.7) | collective-permute-done | bytes 262176 | tf_op jit(solution)/shard_map/ppermute | solution.py:396
  11.9 1.8 %collective-permute-start.8 = (bf16[256,512]{1,0:T(8,128)(2,1)S(1)}, bf16[256,512]{1,0:T(8,128)(2,1)}, u32[]{:S(2)}, u32[]{:S(2)}) collective-permute-start(bf16[256,512]{1,0:T(8,128)(2,1)S(1)} %collective-permute-done.7.refs_4_), channel_id=1, source_target_pairs={{0,8},{8,16},{16,24},{24,28},{28,20},{20,12},{12,4},{4,0},{1,9},{9... | collective-permute-start | bytes 786440 | tf_op jit(solution)/shard_map/ppermute | solution.py:396
  15.3 1.7 %collective-permute-start.15 = (bf16[256,512]{1,0:T(8,128)(2,1)}, bf16[256,512]{1,0:T(8,128)(2,1)S(1)}, u32[]{:S(2)}, u32[]{:S(2)}) collective-permute-start(bf16[256,512]{1,0:T(8,128)(2,1)} %get-tuple-element.76), channel_id=1, source_target_pairs={{28,0},{0,4},{4,8},{8,12},{12,16},{16,20},{20,24},{24,28},{29,1},{... | collective-permute-start | bytes 786440 | tf_op jit(solution)/shard_map/ppermute | solution.py:418
  20.1 1.6 %collective-permute-start.11 = (bf16[256,512]{1,0:T(8,128)(2,1)}, bf16[256,512]{1,0:T(8,128)(2,1)S(1)}, u32[]{:S(2)}, u32[]{:S(2)}) collective-permute-start(bf16[256,512]{1,0:T(8,128)(2,1)} %collective-permute-done.8.refs_3_), channel_id=1, source_target_pairs={{0,8},{8,16},{16,24},{24,28},{28,20},{20,12},{12,4},{4,0},{1,9},{9... | collective-permute-start | bytes 786440 | tf_op jit(solution)/shard_map/ppermute | solution.py:396
  21.6 2.3 %collective-permute-start.12 = (bf16[256,512]{1,0:T(8,128)(2,1)}, bf16[256,512]{1,0:T(8,128)(2,1)S(1)}, u32[]{:S(2)}, u32[]{:S(2)}) collective-permute-start(bf16[256,512]{1,0:T(8,128)(2,1)} %collective-permute-done.10.refs_4_), channel_id=1, source_target_pairs={{8,0},{16,8},{24,16},{28,24},{20,28},{12,20},{4,12},{0,4},{9,1},{1... | collective-permute-start | bytes 786440 | tf_op jit(solution)/shard_map/ppermute | solution.py:397
  25.2 5.0 %collective-permute-done.15.behind_ref = bf16[256,512]{1,0:T(8,128)(2,1)S(1)} collective-permute-done((bf16[256,512]{1,0:T(8,128)(2,1)}, bf16[256,512]{1,0:T(8,128)(2,1)S(1)}, u32[]{:S(2)}, u32[]{:S(2)}) %collective-permute-start.15) | collective-permute-done | bytes 262176 | tf_op jit(solution)/shard_map/ppermute | solution.py:418
  31.3 4.3 %collective-permute-done.behind_ref = bf16[256,512]{1,0:T(8,128)(2,1)S(1)} collective-permute-done((bf16[256,512]{1,0:T(8,128)(2,1)S(1)}, bf16[256,512]{1,0:T(8,128)(2,1)S(1)}, u32[]{:S(2)}, u32[]{:S(2)}) %collective-permute-start) | collective-permute-done | bytes 262176 | tf_op jit(solution)/shard_map/ppermute | solution.py:418
  37.0 2.2 %shard_map.129 = (f32[256,512]{1,0:T(8,128)S(1)}, f32[256,512]{1,0:T(8,128)S(1)}, f32[256,512]{1,0:T(8,128)S(1)}) custom-call(f32[256,512]{1,0:T(8,128)S(1)} %bitcast.21, f32[256,512]{1,0:T(8,128)S(1)} %bitcast.25, f32[256,512]{1,0:T(8,128)S(1)} %bitcast.17, bf16[256,512]{1,0:T(8,128)(2,1)S(1)} %get-tuple-element.77.own_ref.refs_3_, ...), custom_call_target="tpu_custom_call" | custom-call | flops 1207959552 | bytes 3932160 | tf_op jit(solution)/shard_map/pallas_call | solution.py:129
  39.3 2.1 %collective-permute-start.13 = (bf16[128,512]{1,0:T(8,128)(2,1)S(1)}, bf16[128,512]{1,0:T(8,128)(2,1)S(1)}, u32[]{:S(2)}, u32[]{:S(2)}) collective-permute-start(bf16[128,512]{1,0:T(8,128)(2,1)S(1)} %slice.36), channel_id=1, source_target_pairs={{0,8},{8,16},{16,24},{24,28},{28,20},{20,12},{12,4},{4,0},{1,9},{9... | collective-permute-start | bytes 393224 | tf_op jit(solution)/shard_map/ppermute | solution.py:389
  41.6 4.0 %shard_map.130 = (f32[256,512]{1,0:T(8,128)S(1)}, f32[256,512]{1,0:T(8,128)S(1)}, f32[256,512]{1,0:T(8,128)S(1)}) custom-call(f32[256,512]{1,0:T(8,128)S(1)} %bitcast.22, f32[256,512]{1,0:T(8,128)S(1)} %bitcast.26, f32[256,512]{1,0:T(8,128)S(1)} %bitcast.18, bf16[256,512]{1,0:T(8,128)(2,1)} %collective-permute-done.8.refs_3_, ...), custom_call_target="tpu_custom_call" | custom-call | flops 1610612736 | bytes 5767168 | tf_op jit(solution)/shard_map/pallas_call | solution.py:129
  47.4 6.5 %shard_map.132 = (f32[256,512]{1,0:T(8,128)S(1)}, f32[256,512]{1,0:T(8,128)S(1)}, f32[256,512]{1,0:T(8,128)S(1)}, bf16[256,256]{1,0:T(8,128)(2,1)S(1)}) custom-call(f32[256,512]{1,0:T(8,128)S(1)} %bitcast.23, f32[256,512]{1,0:T(8,128)S(1)} %bitcast.27, f32[256,512]{1,0:T(8,128)S(1)} %bitcast.19, f32[256,512]{1,0:T(8,128)S(1)} %get-tuple-element.45.refs_3_, ...), custom_call_target="tpu_custom_call" | custom-call | flops 5033164800 | bytes 5636096 | tf_op jit(solution)/shard_map/pallas_call | solution.py:129
  55.7 4.2 %collective-permute-done.16.refs_1_ = bf16[256,256]{1,0:T(8,128)(2,1)S(1)} collective-permute-done((bf16[256,256]{1,0:T(8,128)(2,1)S(1)}, bf16[256,256]{1,0:T(8,128)(2,1)S(1)}, u32[]{:S(2)}, u32[]{:S(2)}) %collective-permute-start.16) | collective-permute-done | bytes 131104 | tf_op jit(solution)/shard_map/ppermute | solution.py:404
  59.9 2.0 %collective-permute-start.31 = (bf16[256,512]{1,0:T(8,128)(2,1)S(1)}, bf16[256,512]{1,0:T(8,128)(2,1)S(1)}, u32[]{:S(2)}, u32[]{:S(2)}) collective-permute-start(bf16[256,512]{1,0:T(8,128)(2,1)S(1)} %collective-permute-done.30.refs_4_), channel_id=1, source_target_pairs={{0,8},{8,16},{16,24},{24,28},{28,20},{20,12},{12,4},{4,0},{1,9},{9... | collective-permute-start | bytes 786440 | tf_op jit(solution)/shard_map/ppermute | solution.py:396
  65.8 3.2 %collective-permute-done.31.refs_3_ = bf16[256,512]{1,0:T(8,128)(2,1)S(1)} collective-permute-done((bf16[256,512]{1,0:T(8,128)(2,1)S(1)}, bf16[256,512]{1,0:T(8,128)(2,1)S(1)}, u32[]{:S(2)}, u32[]{:S(2)}) %collective-permute-start.31) | collective-permute-done | bytes 262176 | tf_op jit(solution)/shard_map/ppermute | solution.py:396
  69.0 1.6 %collective-permute-start.34 = (bf16[256,512]{1,0:T(8,128)(2,1)S(1)}, bf16[256,512]{1,0:T(8,128)(2,1)S(1)}, u32[]{:S(2)}, u32[]{:S(2)}) collective-permute-start(bf16[256,512]{1,0:T(8,128)(2,1)S(1)} %collective-permute-done.31.refs_3_), channel_id=1, source_target_pairs={{0,8},{8,16},{16,24},{24,28},{28,20},{20,12},{12,4},{4,0},{1,9},{9... | collective-permute-start | bytes 786440 | tf_op jit(solution)/shard_map/ppermute | solution.py:396
  71.0 3.9 %collective-permute-done.19.got_ref = bf16[272,512]{1,0:T(8,128)(2,1)S(1)} collective-permute-done((bf16[272,512]{1,0:T(8,128)(2,1)S(1)}, bf16[272,512]{1,0:T(8,128)(2,1)S(1)}, u32[]{:S(2)}, u32[]{:S(2)}) %collective-permute-start.19) | collective-permute-done | bytes 278560 | tf_op jit(solution)/shard_map/ppermute | solution.py:404
  75.4 6.3 %collective-permute-start.21 = (bf16[272,128]{1,0:T(8,128)(2,1)S(1)}, bf16[272,128]{1,0:T(8,128)(2,1)S(1)}, u32[]{:S(2)}, u32[]{:S(2)}) collective-permute-start(bf16[272,128]{1,0:T(8,128)(2,1)S(1)} %get-tuple-element.60), channel_id=1, source_target_pairs={{16,0},{20,4},{24,8},{28,12},{0,16},{4,20},{8,24},{12,28},{17,1},{... | collective-permute-start | bytes 208904 | tf_op jit(solution)/shard_map/ppermute | solution.py:404
  84.1 1.9 %collective-permute-done.21.rest_1_ = bf16[272,128]{1,0:T(8,128)(2,1)S(1)} collective-permute-done((bf16[272,128]{1,0:T(8,128)(2,1)S(1)}, bf16[272,128]{1,0:T(8,128)(2,1)S(1)}, u32[]{:S(2)}, u32[]{:S(2)}) %collective-permute-start.21) | collective-permute-done | bytes 69664 | tf_op jit(solution)/shard_map/ppermute | solution.py:404
  86.0 2.6 %collective-permute-done.22.rest_2_ = bf16[272,128]{1,0:T(8,128)(2,1)S(1)} collective-permute-done((bf16[272,128]{1,0:T(8,128)(2,1)S(1)}, bf16[272,128]{1,0:T(8,128)(2,1)S(1)}, u32[]{:S(2)}, u32[]{:S(2)}) %collective-permute-start.22) | collective-permute-done | bytes 69664 | tf_op jit(solution)/shard_map/ppermute | solution.py:404
  88.8 2.2 %shard_map.138 = (f32[256,512]{1,0:T(8,128)S(1)}, f32[256,512]{1,0:T(8,128)S(1)}, f32[256,512]{1,0:T(8,128)S(1)}) custom-call(f32[256,512]{1,0:T(8,128)S(1)} %get-tuple-element.63.refs_0_, f32[256,512]{1,0:T(8,128)S(1)} %get-tuple-element.64.refs_1_, f32[256,512]{1,0:T(8,128)S(1)} %get-tuple-element.65.refs_2_, ...), custom_call_target="tpu_custom_call" | custom-call | flops 1207959552 | bytes 3932160 | tf_op jit(solution)/shard_map/pallas_call | solution.py:129
  91.1 2.1 %collective-permute-start.24 = (bf16[256,128]{1,0:T(8,128)(2,1)S(1)}, bf16[256,128]{1,0:T(8,128)(2,1)S(1)}, u32[]{:S(2)}, u32[]{:S(2)}) collective-permute-start(bf16[256,128]{1,0:T(8,128)(2,1)S(1)} %get-tuple-element.62.refs_0_), channel_id=1, source_target_pairs={{8,0},{16,8},{24,16},{28,24},{20,28},{12,20},{4,12},{0,4},{9,1},{1... | collective-permute-start | bytes 196616 | tf_op jit(solution)/shard_map/ppermute | solution.py:397
  93.6 2.9 %shard_map.139 = (f32[256,512]{1,0:T(8,128)S(1)}, f32[256,512]{1,0:T(8,128)S(1)}, f32[256,512]{1,0:T(8,128)S(1)}) custom-call(f32[256,512]{1,0:T(8,128)S(1)} %get-tuple-element.63.refs_0_, f32[256,512]{1,0:T(8,128)S(1)} %get-tuple-element.64.refs_1_, f32[256,512]{1,0:T(8,128)S(1)} %get-tuple-element.65.refs_2_, ...), custom_call_target="tpu_custom_call" | custom-call | flops 1610612736 | bytes 5767168 | tf_op jit(solution)/shard_map/pallas_call | solution.py:129
  98.7 6.9 %shard_map.140 = (f32[1,256,512]{2,1,0:T(8,128)}, f32[1,256,512]{2,1,0:T(8,128)}, f32[1,512,256]{2,1,0:T(8,128)}) custom-call(f32[256,512]{1,0:T(8,128)S(1)} %get-tuple-element.63.refs_0_, f32[256,512]{1,0:T(8,128)S(1)} %get-tuple-element.64.refs_1_, f32[256,512]{1,0:T(8,128)S(1)} %get-tuple-element.65.refs_2_, f32[256,512]{1,0:T(8,128)S(1)} %get-tuple-element.69.refs_3_, ...), custom_call_target="tpu_custom_call" | custom-call | flops 5033164800 | bytes 4980736 | tf_op jit(solution)/shard_map/pallas_call | solution.py:129
  (93 shorter events, 31.0 us)
Async XLA Ops:
  2.6 9.3 %collective-permute-start.7 = (bf16[256,512]{1,0:T(8,128)(2,1)S(1)}, bf16[256,512]{1,0:T(8,128)(2,1)S(1)}, u32[]{:S(2)}, u32[]{:S(2)}) collective-permute-start(bf16[256,512]{1,0:T(8,128)(2,1)S(1)} %get-tuple-element.77.own_ref.refs_3_), channel_id=1, source_target_pairs={{0,8},{8,16},{16,24},{24,28},{28,20},{20,12},{12,4},{4,0},{1,9},{9... | collective-permute-start | bytes 786440 | tf_op jit(solution)/shard_map/ppermute | solution.py:396
  5.6 8.8 %collective-permute-start.9 = (bf16[256,512]{1,0:T(8,128)(2,1)S(1)}, bf16[256,512]{1,0:T(8,128)(2,1)S(1)}, u32[]{:S(2)}, u32[]{:S(2)}) collective-permute-start(bf16[256,512]{1,0:T(8,128)(2,1)S(1)} %get-tuple-element.77.own_ref.refs_3_), channel_id=1, source_target_pairs={{8,0},{16,8},{24,16},{28,24},{20,28},{12,20},{4,12},{0,4},{9,1},{1... | collective-permute-start | bytes 786440 | tf_op jit(solution)/shard_map/ppermute | solution.py:397
  11.9 8.2 %collective-permute-start.8 = (bf16[256,512]{1,0:T(8,128)(2,1)S(1)}, bf16[256,512]{1,0:T(8,128)(2,1)}, u32[]{:S(2)}, u32[]{:S(2)}) collective-permute-start(bf16[256,512]{1,0:T(8,128)(2,1)S(1)} %collective-permute-done.7.refs_4_), channel_id=1, source_target_pairs={{0,8},{8,16},{16,24},{24,28},{28,20},{20,12},{12,4},{4,0},{1,9},{9... | collective-permute-start | bytes 786440 | tf_op jit(solution)/shard_map/ppermute | solution.py:396
  15.3 14.8 %collective-permute-start.15 = (bf16[256,512]{1,0:T(8,128)(2,1)}, bf16[256,512]{1,0:T(8,128)(2,1)S(1)}, u32[]{:S(2)}, u32[]{:S(2)}) collective-permute-start(bf16[256,512]{1,0:T(8,128)(2,1)} %get-tuple-element.76), channel_id=1, source_target_pairs={{28,0},{0,4},{4,8},{8,12},{12,16},{16,20},{20,24},{24,28},{29,1},{... | collective-permute-start | bytes 786440 | tf_op jit(solution)/shard_map/ppermute | solution.py:418
  17.0 18.6 %collective-permute-start = (bf16[256,512]{1,0:T(8,128)(2,1)S(1)}, bf16[256,512]{1,0:T(8,128)(2,1)S(1)}, u32[]{:S(2)}, u32[]{:S(2)}) collective-permute-start(bf16[256,512]{1,0:T(8,128)(2,1)S(1)} %get-tuple-element.77.own_ref.refs_3_), channel_id=1, source_target_pairs={{28,0},{0,4},{4,8},{8,12},{12,16},{16,20},{20,24},{24,28},{29,1},{... | collective-permute-start | bytes 786440 | tf_op jit(solution)/shard_map/ppermute | solution.py:418
  18.6 27.0 %collective-permute-start.4 = (bf16[256,1024]{1,0:T(8,128)(2,1)S(1)}, bf16[256,1024]{1,0:T(8,128)(2,1)S(1)}, u32[]{:S(2)}, u32[]{:S(2)}) collective-permute-start(bf16[256,1024]{1,0:T(8,128)(2,1)S(1)} %copy-done.1), channel_id=1, source_target_pairs={{2,0},{3,1},{0,2},{1,3},{6,4},{7,5},{4,6},{5,7},{10,8},{11,9},{8,1... | collective-permute-start | bytes 1572872 | tf_op jit(solution)/shard_map/ppermute | solution.py:404
  20.1 19.2 %collective-permute-start.11 = (bf16[256,512]{1,0:T(8,128)(2,1)}, bf16[256,512]{1,0:T(8,128)(2,1)S(1)}, u32[]{:S(2)}, u32[]{:S(2)}) collective-permute-start(bf16[256,512]{1,0:T(8,128)(2,1)} %collective-permute-done.8.refs_3_), channel_id=1, source_target_pairs={{0,8},{8,16},{16,24},{24,28},{28,20},{20,12},{12,4},{4,0},{1,9},{9... | collective-permute-start | bytes 786440 | tf_op jit(solution)/shard_map/ppermute | solution.py:396
  21.6 19.7 %collective-permute-start.12 = (bf16[256,512]{1,0:T(8,128)(2,1)}, bf16[256,512]{1,0:T(8,128)(2,1)S(1)}, u32[]{:S(2)}, u32[]{:S(2)}) collective-permute-start(bf16[256,512]{1,0:T(8,128)(2,1)} %collective-permute-done.10.refs_4_), channel_id=1, source_target_pairs={{8,0},{16,8},{24,16},{28,24},{20,28},{12,20},{4,12},{0,4},{9,1},{1... | collective-permute-start | bytes 786440 | tf_op jit(solution)/shard_map/ppermute | solution.py:397
  30.1 23.8 %collective-permute-start.30 = (bf16[256,512]{1,0:T(8,128)(2,1)S(1)}, bf16[256,512]{1,0:T(8,128)(2,1)S(1)}, u32[]{:S(2)}, u32[]{:S(2)}) collective-permute-start(bf16[256,512]{1,0:T(8,128)(2,1)S(1)} %get-tuple-element.78.own_ref.refs_3_), channel_id=1, source_target_pairs={{0,8},{8,16},{16,24},{24,28},{28,20},{20,12},{12,4},{4,0},{1,9},{9... | collective-permute-start | bytes 786440 | tf_op jit(solution)/shard_map/ppermute | solution.py:396
  35.6 18.7 %collective-permute-start.32 = (bf16[256,512]{1,0:T(8,128)(2,1)S(1)}, bf16[256,512]{1,0:T(8,128)(2,1)S(1)}, u32[]{:S(2)}, u32[]{:S(2)}) collective-permute-start(bf16[256,512]{1,0:T(8,128)(2,1)S(1)} %get-tuple-element.78.own_ref.refs_3_), channel_id=1, source_target_pairs={{8,0},{16,8},{24,16},{28,24},{20,28},{12,20},{4,12},{0,4},{9,1},{1... | collective-permute-start | bytes 786440 | tf_op jit(solution)/shard_map/ppermute | solution.py:397
  45.6 16.3 %collective-permute-start.5 = (bf16[256,1024]{1,0:T(8,128)(2,1)S(1)}, bf16[256,1024]{1,0:T(8,128)(2,1)S(1)}, u32[]{:S(2)}, u32[]{:S(2)}) collective-permute-start(bf16[256,1024]{1,0:T(8,128)(2,1)S(1)} %copy-done.1), channel_id=1, source_target_pairs={{1,0},{0,1},{3,2},{2,3},{5,4},{4,5},{7,6},{6,7},{9,8},{8,9},{11,10... | collective-permute-start | bytes 1572872 | tf_op jit(solution)/shard_map/ppermute | solution.py:404
  45.7 9.4 %collective-permute-start.1 = (bf16[256,256]{1,0:T(8,128)(2,1)S(1)}, bf16[256,256]{1,0:T(8,128)(2,1)S(1)}, u32[]{:S(2)}, u32[]{:S(2)}) collective-permute-start(bf16[256,256]{1,0:T(8,128)(2,1)S(1)} %shard_map.127.refs_0_), channel_id=1, source_target_pairs={{2,0},{3,1},{0,2},{1,3},{6,4},{7,5},{4,6},{5,7},{10,8},{11,9},{8,1... | collective-permute-start | bytes 393224 | tf_op jit(solution)/shard_map/ppermute | solution.py:404
  47.2 14.7 %collective-permute-start.6 = (bf16[256,1024]{1,0:T(8,128)(2,1)S(1)}, bf16[256,1024]{1,0:T(8,128)(2,1)S(1)}, u32[]{:S(2)}, u32[]{:S(2)}) collective-permute-start(bf16[256,1024]{1,0:T(8,128)(2,1)S(1)} %collective-permute-done.4.refs_5_), channel_id=1, source_target_pairs={{1,0},{0,1},{3,2},{2,3},{5,4},{4,5},{7,6},{6,7},{9,8},{8,9},{11,10... | collective-permute-start | bytes 1572872 | tf_op jit(solution)/shard_map/ppermute | solution.py:404
  59.9 9.1 %collective-permute-start.31 = (bf16[256,512]{1,0:T(8,128)(2,1)S(1)}, bf16[256,512]{1,0:T(8,128)(2,1)S(1)}, u32[]{:S(2)}, u32[]{:S(2)}) collective-permute-start(bf16[256,512]{1,0:T(8,128)(2,1)S(1)} %collective-permute-done.30.refs_4_), channel_id=1, source_target_pairs={{0,8},{8,16},{16,24},{24,28},{28,20},{20,12},{12,4},{4,0},{1,9},{9... | collective-permute-start | bytes 786440 | tf_op jit(solution)/shard_map/ppermute | solution.py:396
  61.9 8.7 %collective-permute-start.33 = (bf16[256,512]{1,0:T(8,128)(2,1)S(1)}, bf16[256,512]{1,0:T(8,128)(2,1)S(1)}, u32[]{:S(2)}, u32[]{:S(2)}) collective-permute-start(bf16[256,512]{1,0:T(8,128)(2,1)S(1)} %collective-permute-done.32.refs_5_), channel_id=1, source_target_pairs={{8,0},{16,8},{24,16},{28,24},{20,28},{12,20},{4,12},{0,4},{9,1},{1... | collective-permute-start | bytes 786440 | tf_op jit(solution)/shard_map/ppermute | solution.py:397
  64.6 10.3 %collective-permute-start.19 = (bf16[272,512]{1,0:T(8,128)(2,1)S(1)}, bf16[272,512]{1,0:T(8,128)(2,1)S(1)}, u32[]{:S(2)}, u32[]{:S(2)}) collective-permute-start(bf16[272,512]{1,0:T(8,128)(2,1)S(1)} %get-tuple-element.55), channel_id=1, source_target_pairs={{4,0},{0,4},{12,8},{8,12},{20,16},{16,20},{28,24},{24,28},{5,1},{1... | collective-permute-start | bytes 835592 | tf_op jit(solution)/shard_map/ppermute | solution.py:404
  69.0 12.7 %collective-permute-start.34 = (bf16[256,512]{1,0:T(8,128)(2,1)S(1)}, bf16[256,512]{1,0:T(8,128)(2,1)S(1)}, u32[]{:S(2)}, u32[]{:S(2)}) collective-permute-start(bf16[256,512]{1,0:T(8,128)(2,1)S(1)} %collective-permute-done.31.refs_3_), channel_id=1, source_target_pairs={{0,8},{8,16},{16,24},{24,28},{28,20},{20,12},{12,4},{4,0},{1,9},{9... | collective-permute-start | bytes 786440 | tf_op jit(solution)/shard_map/ppermute | solution.py:396
  70.6 11.9 %collective-permute-start.35 = (bf16[256,512]{1,0:T(8,128)(2,1)S(1)}, bf16[256,512]{1,0:T(8,128)(2,1)S(1)}, u32[]{:S(2)}, u32[]{:S(2)}) collective-permute-start(bf16[256,512]{1,0:T(8,128)(2,1)S(1)} %collective-permute-done.33.refs_4_), channel_id=1, source_target_pairs={{8,0},{16,8},{24,16},{28,24},{20,28},{12,20},{4,12},{0,4},{9,1},{1... | collective-permute-start | bytes 786440 | tf_op jit(solution)/shard_map/ppermute | solution.py:397
  75.1 9.0 %collective-permute-start.20 = (bf16[272,128]{1,0:T(8,128)(2,1)S(1)}, bf16[272,128]{1,0:T(8,128)(2,1)S(1)}, u32[]{:S(2)}, u32[]{:S(2)}) collective-permute-start(bf16[272,128]{1,0:T(8,128)(2,1)S(1)} %get-tuple-element.59), channel_id=1, source_target_pairs={{8,0},{12,4},{0,8},{4,12},{24,16},{28,20},{16,24},{20,28},{9,1},{1... | collective-permute-start | bytes 208904 | tf_op jit(solution)/shard_map/ppermute | solution.py:404
  75.4 10.5 %collective-permute-start.21 = (bf16[272,128]{1,0:T(8,128)(2,1)S(1)}, bf16[272,128]{1,0:T(8,128)(2,1)S(1)}, u32[]{:S(2)}, u32[]{:S(2)}) collective-permute-start(bf16[272,128]{1,0:T(8,128)(2,1)S(1)} %get-tuple-element.60), channel_id=1, source_target_pairs={{16,0},{20,4},{24,8},{28,12},{0,16},{4,20},{8,24},{12,28},{17,1},{... | collective-permute-start | bytes 208904 | tf_op jit(solution)/shard_map/ppermute | solution.py:404
  81.7 17.0 %collective-permute-start.36 = (bf16[128,512]{1,0:T(8,128)(2,1)S(1)}, bf16[128,512]{1,0:T(8,128)(2,1)S(1)}, u32[]{:S(2)}, u32[]{:S(2)}) collective-permute-start(bf16[128,512]{1,0:T(8,128)(2,1)S(1)} %slice.38), channel_id=1, source_target_pairs={{0,8},{8,16},{16,24},{24,28},{28,20},{20,12},{12,4},{4,0},{1,9},{9... | collective-permute-start | bytes 393224 | tf_op jit(solution)/shard_map/ppermute | solution.py:389
  82.6 16.1 %collective-permute-start.37 = (bf16[128,512]{1,0:T(8,128)(2,1)S(1)}, bf16[128,512]{1,0:T(8,128)(2,1)S(1)}, u32[]{:S(2)}, u32[]{:S(2)}) collective-permute-start(bf16[128,512]{1,0:T(8,128)(2,1)S(1)} %slice.39), channel_id=1, source_target_pairs={{8,0},{16,8},{24,16},{28,24},{20,28},{12,20},{4,12},{0,4},{9,1},{1... | collective-permute-start | bytes 393224 | tf_op jit(solution)/shard_map/ppermute | solution.py:390
  96.6 9.0 %collective-permute-start.26 = (bf16[256,128]{1,0:T(8,128)(2,1)S(1)}, bf16[256,128]{1,0:T(8,128)(2,1)S(1)}, u32[]{:S(2)}, u32[]{:S(2)}) collective-permute-start(bf16[256,128]{1,0:T(8,128)(2,1)S(1)} %collective-permute-done.24.refs_2_), channel_id=1, source_target_pairs={{8,0},{16,8},{24,16},{28,24},{20,28},{12,20},{4,12},{0,4},{9,1},{1... | collective-permute-start | bytes 196616 | tf_op jit(solution)/shard_map/ppermute | solution.py:397
  98.2 8.9 %collective-permute-start.27 = (bf16[256,128]{1,0:T(8,128)(2,1)S(1)}, bf16[256,128]{1,0:T(8,128)(2,1)S(1)}, u32[]{:S(2)}, u32[]{:S(2)}) collective-permute-start(bf16[256,128]{1,0:T(8,128)(2,1)S(1)} %collective-permute-done.25.refs_3_), channel_id=1, source_target_pairs={{0,8},{8,16},{16,24},{24,28},{28,20},{20,12},{12,4},{4,0},{1,9},{9... | collective-permute-start | bytes 196616 | tf_op jit(solution)/shard_map/ppermute | solution.py:396
  (23 other events, 134.3 us)

commit v2 on v1

v2 whole, which is shorter than its diff:
```python
import functools
import math

import jax
import jax.numpy as jnp
from jax import lax
from jax.experimental import pallas as pl
from jax.experimental.pallas import tpu as pltpu
from jax.sharding import PartitionSpec as P

WINDOW = 256
NS_STEPS = 5
SCHULZ_COEFFS = (3.4445, -4.775, 2.0315)
LEARN_RATE = 0.5
EPSILON = 1e-06
LANES = 128
LOSS_ROWS = 16
VMEM_BYTES = 40 * 1024 * 1024

F32 = jnp.float32
BF16 = jnp.bfloat16


def mm(a, b):
    return jnp.dot(a, b, preferred_element_type=F32)


def mm_nt(a, b):
    return lax.dot_general(a, b, (((1,), (1,)), ((), ())), preferred_element_type=F32)


def mm_tn(a, b):
    return lax.dot_general(a, b, (((0,), (0,)), ((), ())), preferred_element_type=F32)


def split(x):
    high = x.astype(BF16)
    return high, (x - high.astype(F32)).astype(BF16)


def token_gradients(weights, keys, values):
    w_one, w_three, w_two_t = weights
    gate = mm(keys, w_one)
    up = mm(keys, w_three)
    d_hidden = -mm(values, w_two_t)
    sig = jax.nn.sigmoid(gate)
    silu = gate * sig
    d_gate = d_hidden * up * sig * (1.0 + gate * (1.0 - sig))
    d_up = d_hidden * silu
    hidden = silu * up
    return (
        mm_tn(keys, d_gate.astype(BF16)),
        mm_tn(keys, d_up.astype(BF16)),
        -mm_tn(values, hidden.astype(BF16)),
    )


def orthogonalize(mats):
    a, b, c = SCHULZ_COEFFS
    centre = -b / (2.0 * c)
    rest = a - b * b / (4.0 * c)
    rows = mats[0].shape[0]
    shape = (rows, rows)
    diag = lax.broadcasted_iota(jnp.int32, shape, 0) == lax.broadcasted_iota(jnp.int32, shape, 1)
    xs = [m * (1.0 / (jnp.sqrt(jnp.sum(m * m)) + EPSILON)) for m in mats]
    for sweep in range(NS_STEPS):
        if sweep < 2:
            lows = [x.astype(BF16) for x in xs]
            grams = [mm_nt(x, x) for x in lows]
            halves = [g.astype(BF16) for g in grams]
            polys = [(b * g + c * mm(h, h)).astype(BF16) for g, h in zip(grams, halves)]
            xs = [a * x + mm(p, low) for x, p, low in zip(xs, polys, lows)]
        elif sweep == 2:
            pairs = [split(x) for x in xs]
            grams = [mm_nt(h, h) + mm_nt(h, l) + mm_nt(l, h) for h, l in pairs]
            gpairs = [split(g) for g in grams]
            polys = [
                b * g + c * (mm(h, h) + mm(h, l) + mm(l, h)) for g, (h, l) in zip(grams, gpairs)
            ]
            ppairs = [split(p) for p in polys]
            xs = [
                a * x + (mm(ph, h) + mm(ph, l) + mm(pl_, h))
                for x, (ph, pl_), (h, l) in zip(xs, ppairs, pairs)
            ]
        else:
            lows = [x.astype(BF16) for x in xs]
            grams = [mm_nt(x, x) for x in lows]
            moved = [jnp.where(diag, g - centre, g).astype(BF16) for g in grams]
            polys = [(c * mm(h, h)).astype(BF16) for h in moved]
            xs = [rest * x + mm(p, low) for x, p, low in zip(xs, polys, lows)]
    return xs


def normed_forward(weights, queries):
    w_one, w_three, w_two_t = [split(w) for w in weights]
    gate = mm(queries, w_one[0]) + mm(queries, w_one[1])
    up = mm(queries, w_three[0]) + mm(queries, w_three[1])
    hidden = (gate * jax.nn.sigmoid(gate) * up).astype(BF16)
    out = mm_nt(hidden, w_two_t[0]) + mm_nt(hidden, w_two_t[1])
    return out * lax.rsqrt(jnp.mean(out * out, axis=-1, keepdims=True) + EPSILON)


def window_attention(queries, own, behind, has_behind):
    tok, width = queries.shape
    head_dim = width
    scale = 1.0 / math.sqrt(head_dim)
    shape = (tok, tok)
    row = lax.broadcasted_iota(jnp.int32, shape, 0)
    col = lax.broadcasted_iota(jnp.int32, shape, 1)
    allow_own = (row >= col) & (row - col < WINDOW)
    allow_behind = (row + tok - col < WINDOW) & has_behind
    s_own = jnp.where(allow_own, mm_nt(queries, own[:, :width]) * scale, -1e30)
    s_behind = jnp.where(allow_behind, mm_nt(queries, behind[:, :width]) * scale, -1e30)
    top = jnp.maximum(
        jnp.max(s_own, axis=1, keepdims=True), jnp.max(s_behind, axis=1, keepdims=True)
    )
    e_own = jnp.where(allow_own, jnp.exp(s_own - top), 0.0)
    e_behind = jnp.where(allow_behind, jnp.exp(s_behind - top), 0.0)
    total = jnp.sum(e_own, axis=1, keepdims=True) + jnp.sum(e_behind, axis=1, keepdims=True)
    inv = 1.0 / total
    return mm((e_own * inv).astype(BF16), own[:, width:]) + mm(
        (e_behind * inv).astype(BF16), behind[:, width:]
    )


def call(kernel, outs, args, flops=0, scratch=()):
    vmem = pl.BlockSpec(memory_space=pltpu.VMEM)
    size = sum(math.prod(a.shape) * a.dtype.itemsize for a in list(args) + list(outs))
    return pl.pallas_call(
        kernel,
        out_shape=tuple(jax.ShapeDtypeStruct(o.shape, o.dtype) for o in outs),
        in_specs=[vmem] * len(args),
        out_specs=tuple([vmem] * len(outs)),
        scratch_shapes=list(scratch),
        compiler_params=pltpu.CompilerParams(vmem_limit_bytes=VMEM_BYTES),
        cost_estimate=pl.CostEstimate(flops=flops, bytes_accessed=size, transcendentals=0),
    )(*args)


def like(shape, dtype):
    return jax.ShapeDtypeStruct(shape, dtype)


def gradients(weights, runs, before):
    rows, hidden = weights[0].shape
    count = len(runs)

    def kernel(*refs):
        w = [r[...].astype(BF16) for r in refs[:3]]
        run_refs = refs[3 : 3 + count]
        prev = refs[3 + count : -3]
        sums = [p[...] for p in prev] if prev else None
        for run in run_refs:
            new = token_gradients(w, run[:, :rows], run[:, rows:])
            sums = list(new) if sums is None else [s + n for s, n in zip(sums, new)]
        for out, value in zip(refs[-3:], sums):
            out[...] = value

    tokens = sum(r.shape[0] for r in runs)
    args = list(weights) + list(runs) + (list(before) if before is not None else [])
    outs = [like((rows, hidden), F32)] * 3
    return call(kernel, outs, args, flops=12 * tokens * rows * hidden)


def update(weights, grads, last_runs, queries=None, block=None):
    rows, hidden = weights[0].shape
    count = len(last_runs)
    mixes = queries is not None

    def kernel(*refs):
        w = [r[...] for r in refs[:3]]
        sums = [r[...] for r in refs[3:6]]
        run_refs = refs[6 : 6 + count]
        low = [x.astype(BF16) for x in w]
        for run in run_refs:
            new = token_gradients(low, run[:, :rows], run[:, rows:])
            sums = [s + n for s, n in zip(sums, new)]
        ortho = orthogonalize(sums)
        fresh = [x - LEARN_RATE * o for x, o in zip(w, ortho)]
        if mixes:
            q_ref = refs[6 + count]
            outs = refs[7 + count :]
            for out, value in zip(outs, fresh):
                out[...] = value
            outs[3][...] = normed_forward(fresh, q_ref[block])
        else:
            outs = refs[6 + count :]
            outs[0][0] = fresh[0]
            outs[1][0] = fresh[1]
            outs[2][0] = fresh[2].T

    args = list(weights) + list(grads) + list(last_runs)
    if mixes:
        args += [queries]
        outs = [like((rows, hidden), F32)] * 3 + [like(queries.shape[1:], F32)]
    else:
        outs = [like((1, rows, hidden), F32)] * 2 + [like((1, hidden, rows), F32)]
    flops = 3 * 5 * 2 * (2 * rows * rows * hidden + rows**3) * 2
    return call(kernel, outs, args, flops=flops)


def later_mix(queries, own, behind, normed, block):
    def kernel(q_ref, own_ref, behind_ref, normed_ref, out_ref):
        has_behind = (lax.axis_index("seq") > 0) | (block > 0)
        att = window_attention(q_ref[block], own_ref[...], behind_ref[...], has_behind)
        out_ref[...] = (att + normed_ref[...]).astype(BF16)

    tok, width = queries.shape[1:]
    return call(
        kernel,
        [like((tok, width), BF16)],
        [queries, own, behind, normed],
        flops=8 * tok * tok * width,
    )[0]


def first_mix(queries, own, others, tables, weights):
    count = len(others)

    def kernel(q_ref, own_ref, *refs):
        other_refs = refs[:count]
        one_ref, three_ref, two_ref, out_ref, behind_ref = refs[count:]
        me = lax.axis_index("seq")
        behind_ref[...] = own_ref[...]
        for ref, (table, first_row) in zip(other_refs, tables):
            owner = sum(jnp.where(me == d, o, 0) for d, o in enumerate(table))

            @pl.when(owner == me - 1)
            def _():
                behind_ref[first_row : first_row + ref.shape[0], :] = ref[...]

        queries = q_ref[0]
        att = window_attention(queries, own_ref[...], behind_ref[...], me > 0)
        w = [one_ref[...], three_ref[...], two_ref[...]]
        out_ref[...] = (att + normed_forward(w, queries)).astype(BF16)

    tok, width = queries.shape[1:]
    return call(
        kernel,
        [like((tok, width), BF16)],
        [queries, own] + list(others) + list(weights),
        flops=20 * tok * tok * width,
        scratch=[pltpu.VMEM(own.shape, BF16)],
    )[0]


def loss_tile(loss):
    high = loss.astype(BF16).astype(F32)
    row = lax.broadcasted_iota(jnp.int32, (LOSS_ROWS, LANES), 0)
    return jnp.where(row < LOSS_ROWS // 2, high, loss - high).astype(BF16)


def tile_loss(tile):
    return jnp.sum(tile.astype(F32)) * (1.0 / (LOSS_ROWS // 2 * LANES))


def project(mixed_parts, proj_parts, teacher, block, before, chunks):
    count = len(mixed_parts)
    tok, width = mixed_parts[0].shape
    cols = teacher.shape[2]
    extra = [] if before is None else list(before)
    chunk = cols // max(chunks, 1)

    def kernel(*refs):
        mixed_refs, proj_refs = refs[:count], refs[count : 2 * count]
        teacher_ref = refs[2 * count]
        before_refs = refs[2 * count + 1 : 2 * count + 1 + len(extra)]
        outs = refs[2 * count + 1 + len(extra) :]
        student_ref, term_ref, loss_ref = outs[:3]
        low_ref = outs[-2] if chunks else outs[-1]
        full_ref = outs[-1] if chunks else term_ref
        summed = mm(mixed_refs[0][...], proj_refs[0][...])
        for m, p in zip(mixed_refs[1:], proj_refs[1:]):
            summed = summed + mm(m[...], p[...])
        low_ref[...] = summed.astype(BF16)
        start = pl.multiple_of(lax.axis_index("head") * width, width)
        student_ref[...] = low_ref[:, pl.ds(start, width)]
        diff = summed - teacher_ref[block].astype(F32)
        term = mm_tn(mixed_refs[0][...], diff.astype(BF16))
        loss = jnp.sum(diff * diff)
        if before_refs:
            term = term + before_refs[0][...]
            loss = loss + jnp.max(before_refs[1][...])
        full_ref[...] = term
        loss_ref[...] = jnp.full((8, LANES), loss, F32)
        if chunks:
            place = lax.axis_index("seq")
            tile = loss_tile(loss)

            def part(index):
                return full_ref[:, pl.ds(pl.multiple_of(index * chunk, chunk), chunk)]

            term_ref[...] = part(place)
            for offset, send in enumerate(outs[3:-2], start=1):
                send[:width, :] = part(place ^ offset).astype(BF16)
                for at in range(0, chunk, LANES):
                    send[width:, at : at + LANES] = tile

    outs = [like((tok, width), BF16), like((width, chunk), F32), like((8, LANES), F32)]
    outs += [like((width + LOSS_ROWS, chunk), BF16)] * max(chunks - 1, 0)
    scratch = [pltpu.VMEM((tok, cols), BF16)]
    if chunks:
        scratch.append(pltpu.VMEM((width, cols), F32))
    return call(
        kernel,
        outs,
        list(mixed_parts) + list(proj_parts) + [teacher] + extra,
        flops=2 * tok * cols * width * (count + 1),
        scratch=scratch,
    )


def outer_total(own, loss, gots, grad_scale, loss_scale):
    width, chunk = own.shape

    def kernel(own_ref, loss_ref, *rest):
        got_refs, out_ref, new_loss_ref = rest[:-2], rest[-2], rest[-1]
        total = own_ref[...]
        sq = jnp.max(loss_ref[...])
        for got in got_refs:
            total = total + got[:width, :].astype(F32)
            sq = sq + tile_loss(got[width:, :LANES])
        out_ref[...] = (total * grad_scale).astype(BF16)
        new_loss_ref[...] = jnp.full((8, LANES), sq * loss_scale, F32)

    return call(
        kernel, [like((width, chunk), BF16), like((8, LANES), F32)], [own, loss] + list(gots)
    )


def assemble(pieces, offsets, cols):
    width, chunk = pieces[0].shape
    count = len(pieces)

    def kernel(*refs):
        out_ref = refs[-1]
        me = lax.axis_index("seq")
        for ref, offset in zip(refs[:count], offsets):
            start = pl.multiple_of((me ^ offset) * chunk, chunk)
            out_ref[:, pl.ds(start, chunk)] = ref[...].astype(F32)

    return call(kernel, [like((width, cols), F32)], list(pieces))[0]


def ring_order(size):
    return list(range(0, size, 2)) + list(range(size - 1 - size % 2, 0, -2))


class Ring:
    def __init__(self, block, axis):
        size = lax.axis_size(axis)
        self.block, self.axis, self.size = block, axis, size
        self.order = ring_order(size)
        self.ahead = [(self.order[i], self.order[(i + 1) % size]) for i in range(size)]
        self.back = [(b, a) for a, b in self.ahead]
        self.up = self.down = block
        self.done = 0
        self.got = []

    def source(self, distance):
        table = [0] * self.size
        for i, d in enumerate(self.order):
            table[d] = self.order[(i - distance) % self.size]
        return table

    def step(self, *earlier):
        self.done += 1
        up, down = after(self.up, *earlier), after(self.down, *earlier)
        if 2 * self.done == self.size:
            rows = self.block.shape[0] // 2
            one = lax.ppermute(up[:rows], self.axis, self.ahead)
            two = lax.ppermute(down[rows:], self.axis, self.back)
            self.got += [(one, self.source(self.done), 0), (two, self.source(self.done), rows)]
            return [one, two]
        self.up = lax.ppermute(up, self.axis, self.ahead)
        self.down = lax.ppermute(down, self.axis, self.back)
        self.got += [(self.up, self.source(self.done), 0), (self.down, self.source(-self.done), 0)]
        return [self.up, self.down]


def partner(block, axis, bit):
    size = lax.axis_size(axis)
    return lax.ppermute(block, axis, [(i ^ bit, i) for i in range(size)])


def cube_gather(block, axis):
    parts = [block]
    bit = lax.axis_size(axis) // 2
    while bit:
        parts += [partner(p, axis, bit) for p in parts]
        bit //= 2
    return parts


def from_behind(block, axis):
    size = lax.axis_size(axis)
    return lax.ppermute(block, axis, [((i - 1) % size, i) for i in range(size)])


def after(value, *earlier):
    return lax.optimization_barrier((value,) + earlier)[0]


def local(query_rows, key_rows, value_rows, first_fast, third_fast, second_fast, out_proj, teacher):
    block_count, tok, head_dim = query_rows.shape
    seq = lax.axis_size("seq")
    cols = out_proj.shape[1]
    total_rows = block_count * tok * seq
    pos = lax.axis_index("seq")
    gathers = seq <= 8 and seq % 2 == 0
    grad_scale = 1.0 / math.sqrt(total_rows)
    loss_scale = 1.0 / (total_rows * cols)
    weights = (first_fast[0], third_fast[0], second_fast[0].T)

    kv = [jnp.concatenate([key_rows[c], value_rows[c]], axis=1) for c in range(block_count)]
    rims = [kv[0]] + [jnp.where(pos == seq - 1, kv[c - 1], kv[c]) for c in range(1, block_count)]

    def ring_gradients(ring, weights, runs, *earlier):
        grads = None
        runs = [after(ring.block, *earlier)] + runs
        while 2 * ring.done < ring.size:
            later = ring.step(*(grads or ())[:1])
            grads = gradients(weights, runs, grads)
            runs = later
        return grads, runs

    mixed = []
    history = [weights]
    rings = []
    proj_parts = None
    if gathers:
        earlier = ()
        for c in range(block_count - 1):
            ring = Ring(after(kv[c], *earlier), "seq")
            rings.append(ring)
            runs = ring.step()
            if proj_parts is None:
                proj_parts = cube_gather(after(out_proj, runs[0]), "head")
            grads, final = ring_gradients(ring, weights, runs)
            earlier = (ring.up, ring.down)
            behind = from_behind(after(rims[c + 1], *earlier), "seq")
            if c + 2 == block_count:
                last_ring = Ring(after(kv[c + 1], *earlier), "seq")
                last_runs = last_ring.step()
            *fresh, normed = update(weights, grads, final, query_rows, c + 1)
            weights = tuple(fresh)
            history.append(weights)
            mixed.append(later_mix(query_rows, kv[c + 1], behind, normed, c + 1))
        others = [block for block, _, _ in rings[0].got]
        tables = [(table, row) for _, table, row in rings[0].got]
    else:
        proj_parts = cube_gather(out_proj, "head")
        for c in range(block_count - 1):
            grads = lax.psum(gradients(weights, [kv[c]], None), "seq")
            behind = from_behind(rims[c + 1], "seq")
            *fresh, normed = update(weights, grads, [], query_rows, c + 1)
            weights = tuple(fresh)
            history.append(weights)
            mixed.append(later_mix(query_rows, kv[c + 1], behind, normed, c + 1))
        others = [from_behind(rims[0], "seq")]
        tables = [([(d - 1) % seq for d in range(seq)], 0)]
    mixed.insert(0, first_mix(query_rows, after(kv[0], *mixed[-1:]), others, tables, history[0]))

    chunks = seq if gathers and seq & (seq - 1) == 0 and cols % (seq * LANES) == 0 else 0
    students = [None] * block_count
    before = None
    if gathers:
        mixed[-1] = after(mixed[-1], *last_runs)
    for c in range(block_count):
        last = c + 1 == block_count
        parts = cube_gather(mixed[c], "head")
        if last and gathers:
            grads = gradients(weights, [kv[c]] + last_runs, None)
            next_runs = last_ring.step()
            parts[-1] = after(parts[-1], *next_runs)
        students[c], *rest = project(
            parts, proj_parts, teacher, c, before, chunks if last else 0
        )
        before = rest
    term, loss, *sends = before

    if gathers:
        while 2 * last_ring.done < seq:
            runs, next_runs = next_runs, last_ring.step()
            grads = gradients(weights, runs, grads)
        final = next_runs
    else:
        grads, final = lax.psum(gradients(weights, [kv[-1]], None), "seq"), []
    new_first, new_third, new_second = update(weights, grads, final)

    if chunks:
        gots = [partner(s, "seq", m) for m, s in enumerate(sends, start=1)]
        term = after(term, *final)
        piece, loss = outer_total(term, loss, gots, grad_scale, loss_scale)
        line = [(2 * m, partner(piece, "seq", 2 * m)) for m in range(1, seq // 2)]
        pieces = [(0, piece)] + line
        pieces += [(m + 1, partner(p, "seq", 1)) for m, p in pieces]
        out_grad = assemble([p for _, p in pieces], [m for m, _ in pieces], cols)
        distill_loss = loss[0, 0]
    else:
        term, loss = lax.psum((term, loss), "seq")
        out_grad = term * grad_scale
        distill_loss = loss[0, 0] * loss_scale
    return (jnp.stack(students), out_grad, new_first, new_third, new_second, distill_loss)


def solution(mesh):
    in_specs = (
        P(None, "seq", "head"),
        P(None, "seq", "head"),
        P(None, "seq", "head"),
        P("head", None, None),
        P("head", None, None),
        P("head", None, None),
        P("head", None),
        P(None, "seq", None),
    )
    out_specs = (
        P(None, "seq", "head"),
        P("head", None),
        P("head", None, None),
        P("head", None, None),
        P("head", None, None),
        P(),
    )
    return jax.shard_map(local, mesh=mesh, in_specs=in_specs, out_specs=out_specs, check_vma=False)
```

time: 113 us -> 100 us (0.88)
  waiting for transfers between devices: 34.1 us -> 24.9 us
  local copies, waits for them, and re-layouts: 4.35 us -> 2.94 us
  Pallas kernels: 30.9 us -> 29.7 us
    ppermute x13 -> x23, starting transfers between devices: 12.6 us -> 24.5 us  [partner(): return lax.ppermute(block, axis, [(i ^ bit, i) for i in range(size)])]
    ppermute x23 -> x16, starting transfers between devices: 24.9 us -> 15.9 us  [the longest x6 9.51 us: step(): self.up = lax.ppermute(up, self.axis, self.ahead)]
    ppermute x2 -> x1, waiting for transfers between devices: 9.23 us -> 1.89 us  [from_behind(): return lax.ppermute(block, axis, [((i - 1) % size, i) for i in range(size)])]
    ppermute x13 -> x23, waiting for transfers between devices: 12.8 us -> 7.35 us  [partner(): return lax.ppermute(block, axis, [(i ^ bit, i) for i in range(size)])]
    ppermute x23 -> x16, waiting for transfers between devices: 12 us -> 15.6 us  [the longest x6 13.6 us: step(): self.up = lax.ppermute(up, self.axis, self.ahead)]
    ppermute x2 -> x1, starting transfers between devices: 3.26 us -> 0.6 us  [from_behind(): return lax.ppermute(block, axis, [((i - 1) % size, i) for i in range(size)])]
    unnamed x19 -> x11, local copies, waits for them, and re-layouts: 2.67 us -> 1.26 us
    pallas_call x14, Pallas kernels: 30.9 us -> 29.7 us  [call(): pl.pallas_call(kernel, out_shape=tuple((jax.ShapeDtypeStruct(o.shape, o.d...]
  transfers between devices with their start and end apart: 38 -> 40, of which waited for: 11 -> 14; matrix products, arithmetic and copies ran while one was open for 2% -> 3% of each run, Pallas kernels for 26% -> 28%
where the time goes in v2:
time: 100 us
  starting transfers between devices  41 us (41%)
  Pallas kernels  29.7 us (30%)
  waiting for transfers between devices  24.9 us (25%)
  local copies, waits for them, and re-layouts  2.94 us (3%)
    pallas_call x14, Pallas kernels, call(): pl.pallas_call(kernel, out_shape=tuple((jax.ShapeDtypeStruct(o.shape, o.d...  29.7 us
    ppermute x23, starting transfers between devices, partner(): return lax.ppermute(block, axis, [(i ^ bit, i) for i in range(size)])  24.5 us
    ppermute x6, waiting for transfers between devices, step(): self.up = lax.ppermute(up, self.axis, self.ahead)  13.6 us
    ppermute x6, starting transfers between devices, step(): self.up = lax.ppermute(up, self.axis, self.ahead)  9.51 us
    ppermute x23, waiting for transfers between devices, partner(): return lax.ppermute(block, axis, [(i ^ bit, i) for i in range(size)])  7.35 us
    ppermute x2, starting transfers between devices, step(): two = lax.ppermute(down[rows:], self.axis, self.back)  2.51 us
  transfers between devices with their start and end apart: 40, of which 14 were waited for; matrix products, arithmetic and copies ran while one was open for 3% of the time, Pallas kernels for 28%

profile of v2, /device:TPU:0, one launch (start us, length us, event | category | flops | bytes accessed | tf_op | source)
XLA Modules:
  0.0 100.2 jit_solution(17844531291842138897)
XLA Ops:
  1.9 3.1 %collective-permute-start = (bf16[256,512]{1,0:T(8,128)(2,1)S(1)}, bf16[256,512]{1,0:T(8,128)(2,1)S(1)}, u32[]{:S(2)}, u32[]{:S(2)}) collective-permute-start(bf16[256,512]{1,0:T(8,128)(2,1)S(1)} %get-tuple-element.72.refs_3_.own_ref), channel_id=1, source_target_pairs={{0,8},{8,16},{16,24},{24,28},{28,20},{20,12},{12,4},{4,0},{1,9},{9... | collective-permute-start | bytes 786440 | tf_op jit(solution)/shard_map/ppermute | solution.py:375
  5.0 6.2 %collective-permute-done.refs_4_.refs_0_ = bf16[256,512]{1,0:T(8,128)(2,1)S(1)} collective-permute-done((bf16[256,512]{1,0:T(8,128)(2,1)S(1)}, bf16[256,512]{1,0:T(8,128)(2,1)S(1)}, u32[]{:S(2)}, u32[]{:S(2)}) %collective-permute-start) | collective-permute-done | bytes 262176 | tf_op jit(solution)/shard_map/ppermute | solution.py:375
  11.2 1.8 %collective-permute-start.1 = (bf16[256,512]{1,0:T(8,128)(2,1)S(1)}, bf16[256,512]{1,0:T(8,128)(2,1)S(1)}, u32[]{:S(2)}, u32[]{:S(2)}) collective-permute-start(bf16[256,512]{1,0:T(8,128)(2,1)S(1)} %collective-permute-done.refs_4_.refs_0_), channel_id=1, source_target_pairs={{0,8},{8,16},{16,24},{24,28},{28,20},{20,12},{12,4},{4,0},{1,9},{9... | collective-permute-start | bytes 786440 | tf_op jit(solution)/shard_map/ppermute | solution.py:375
  14.5 2.2 %shard_map.127 = (f32[256,512]{1,0:T(8,128)S(1)}, f32[256,512]{1,0:T(8,128)S(1)}, f32[256,512]{1,0:T(8,128)S(1)}) custom-call(f32[256,512]{1,0:T(8,128)S(1)} %bitcast.21, f32[256,512]{1,0:T(8,128)S(1)} %bitcast.26, f32[256,512]{1,0:T(8,128)S(1)} %bitcast.16, bf16[256,512]{1,0:T(8,128)(2,1)S(1)} %get-tuple-element.72.refs_3_.own_ref, ...), custom_call_target="tpu_custom_call" | custom-call | flops 1207959552 | bytes 3932160 | tf_op jit(solution)/shard_map/pallas_call | solution.py:129
  16.8 1.9 %collective-permute-done.1.refs_3_.refs_2_ = bf16[256,512]{1,0:T(8,128)(2,1)S(1)} collective-permute-done((bf16[256,512]{1,0:T(8,128)(2,1)S(1)}, bf16[256,512]{1,0:T(8,128)(2,1)S(1)}, u32[]{:S(2)}, u32[]{:S(2)}) %collective-permute-start.1) | collective-permute-done | bytes 262176 | tf_op jit(solution)/shard_map/ppermute | solution.py:375
  22.1 3.1 %collective-permute-done.3.refs_3_.refs_4_ = bf16[256,512]{1,0:T(8,128)(2,1)S(1)} collective-permute-done((bf16[256,512]{1,0:T(8,128)(2,1)S(1)}, bf16[256,512]{1,0:T(8,128)(2,1)S(1)}, u32[]{:S(2)}, u32[]{:S(2)}) %collective-permute-start.3) | collective-permute-done | bytes 262176 | tf_op jit(solution)/shard_map/ppermute | solution.py:375
  30.1 1.6 %collective-permute-start.7 = (bf16[128,512]{1,0:T(8,128)(2,1)S(1)}, bf16[128,512]{1,0:T(8,128)(2,1)S(1)}, u32[]{:S(2)}, u32[]{:S(2)}) collective-permute-start(bf16[128,512]{1,0:T(8,128)(2,1)S(1)} %slice.31), channel_id=1, source_target_pairs={{0,8},{8,16},{16,24},{24,28},{28,20},{20,12},{12,4},{4,0},{1,9},{9... | collective-permute-start | bytes 393224 | tf_op jit(solution)/shard_map/ppermute | solution.py:371
  35.1 1.6 %collective-permute-start.20 = (bf16[256,512]{1,0:T(8,128)(2,1)S(1)}, bf16[256,512]{1,0:T(8,128)(2,1)S(1)}, u32[]{:S(2)}, u32[]{:S(2)}) collective-permute-start(bf16[256,512]{1,0:T(8,128)(2,1)S(1)} %collective-permute-done.15.refs_4_), channel_id=1, source_target_pairs={{0,8},{8,16},{16,24},{24,28},{28,20},{20,12},{12,4},{4,0},{1,9},{9... | collective-permute-start | bytes 786440 | tf_op jit(solution)/shard_map/ppermute | solution.py:375
  37.4 6.5 %shard_map.130 = (f32[256,512]{1,0:T(8,128)S(1)}, f32[256,512]{1,0:T(8,128)S(1)}, f32[256,512]{1,0:T(8,128)S(1)}, f32[256,256]{1,0:T(8,128)S(1)}) custom-call(f32[256,512]{1,0:T(8,128)S(1)} %bitcast.24, f32[256,512]{1,0:T(8,128)S(1)} %bitcast.29, f32[256,512]{1,0:T(8,128)S(1)} %bitcast.19, f32[256,512]{1,0:T(8,128)S(1)} %get-tuple-element.66.refs_3_, ...), custom_call_target="tpu_custom_call" | custom-call | flops 5033164800 | bytes 5505024 | tf_op jit(solution)/shard_map/pallas_call | solution.py:129
  43.9 1.9 %collective-permute-done.6.behind_ref = bf16[256,512]{1,0:T(8,128)(2,1)S(1)} collective-permute-done((bf16[256,512]{1,0:T(8,128)(2,1)S(1)}, bf16[256,512]{1,0:T(8,128)(2,1)S(1)}, u32[]{:S(2)}, u32[]{:S(2)}) %collective-permute-start.6) | collective-permute-done | bytes 262176 | tf_op jit(solution)/shard_map/ppermute | solution.py:397
  50.1 1.9 %collective-permute-done.17.refs_1_ = bf16[256,256]{1,0:T(8,128)(2,1)S(1)} collective-permute-done((bf16[256,256]{1,0:T(8,128)(2,1)S(1)}, bf16[256,256]{1,0:T(8,128)(2,1)S(1)}, u32[]{:S(2)}, u32[]{:S(2)}) %collective-permute-start.17) | collective-permute-done | bytes 131104 | tf_op jit(solution)/shard_map/ppermute | solution.py:383
  52.5 2.0 %collective-permute-done.9.refs_1_ = bf16[256,256]{1,0:T(8,128)(2,1)S(1)} collective-permute-done((bf16[256,256]{1,0:T(8,128)(2,1)S(1)}, bf16[256,256]{1,0:T(8,128)(2,1)S(1)}, u32[]{:S(2)}, u32[]{:S(2)}) %collective-permute-start.9) | collective-permute-done | bytes 131104 | tf_op jit(solution)/shard_map/ppermute | solution.py:383
  55.1 2.3 %shard_map.137 = (f32[256,512]{1,0:T(8,128)S(1)}, f32[256,512]{1,0:T(8,128)S(1)}, f32[256,512]{1,0:T(8,128)S(1)}) custom-call(f32[256,512]{1,0:T(8,128)S(1)} %get-tuple-element.92.refs_0_, f32[256,512]{1,0:T(8,128)S(1)} %get-tuple-element.93.refs_1_, f32[256,512]{1,0:T(8,128)S(1)} %get-tuple-element.94.refs_2_, ...), custom_call_target="tpu_custom_call" | custom-call | flops 1207959552 | bytes 3932160 | tf_op jit(solution)/shard_map/pallas_call | solution.py:129
  58.5 2.3 %collective-permute-done.22.refs_3_ = bf16[256,512]{1,0:T(8,128)(2,1)S(1)} collective-permute-done((bf16[256,512]{1,0:T(8,128)(2,1)S(1)}, bf16[256,512]{1,0:T(8,128)(2,1)S(1)}, u32[]{:S(2)}, u32[]{:S(2)}) %collective-permute-start.22) | collective-permute-done | bytes 262176 | tf_op jit(solution)/shard_map/ppermute | solution.py:375
  61.2 2.0 %collective-permute-start.25 = (bf16[128,512]{1,0:T(8,128)(2,1)S(1)}, bf16[128,512]{1,0:T(8,128)(2,1)S(1)}, u32[]{:S(2)}, u32[]{:S(2)}) collective-permute-start(bf16[128,512]{1,0:T(8,128)(2,1)S(1)} %slice.37), channel_id=1, source_target_pairs={{8,0},{16,8},{24,16},{28,24},{20,28},{12,20},{4,12},{0,4},{9,1},{1... | collective-permute-start | bytes 393224 | tf_op jit(solution)/shard_map/ppermute | solution.py:372
  66.0 1.9 %collective-permute-start.28 = (bf16[272,128]{1,0:T(8,128)(2,1)S(1)}, bf16[272,128]{1,0:T(8,128)(2,1)S(1)}, u32[]{:S(2)}, u32[]{:S(2)}) collective-permute-start(bf16[272,128]{1,0:T(8,128)(2,1)S(1)} %get-tuple-element.86), channel_id=1, source_target_pairs={{12,0},{8,4},{4,8},{0,12},{28,16},{24,20},{20,24},{16,28},{13,1},{... | collective-permute-start | bytes 208904 | tf_op jit(solution)/shard_map/ppermute | solution.py:383
  70.1 2.4 %collective-permute-start.30 = (bf16[272,128]{1,0:T(8,128)(2,1)S(1)}, bf16[272,128]{1,0:T(8,128)(2,1)S(1)}, u32[]{:S(2)}, u32[]{:S(2)}) collective-permute-start(bf16[272,128]{1,0:T(8,128)(2,1)S(1)} %get-tuple-element.88), channel_id=1, source_target_pairs={{20,0},{16,4},{28,8},{24,12},{4,16},{0,20},{12,24},{8,28},{21,1},{... | collective-permute-start | bytes 208904 | tf_op jit(solution)/shard_map/ppermute | solution.py:383
  72.5 1.7 %collective-permute-start.31 = (bf16[272,128]{1,0:T(8,128)(2,1)S(1)}, bf16[272,128]{1,0:T(8,128)(2,1)S(1)}, u32[]{:S(2)}, u32[]{:S(2)}) collective-permute-start(bf16[272,128]{1,0:T(8,128)(2,1)S(1)} %get-tuple-element.89), channel_id=1, source_target_pairs={{24,0},{28,4},{16,8},{20,12},{8,16},{12,20},{0,24},{4,28},{25,1},{... | collective-permute-start | bytes 208904 | tf_op jit(solution)/shard_map/ppermute | solution.py:383
  74.2 2.9 %collective-permute-start.32 = (bf16[272,128]{1,0:T(8,128)(2,1)S(1)}, bf16[272,128]{1,0:T(8,128)(2,1)S(1)}, u32[]{:S(2)}, u32[]{:S(2)}) collective-permute-start(bf16[272,128]{1,0:T(8,128)(2,1)S(1)} %get-tuple-element.90), channel_id=1, source_target_pairs={{28,0},{24,4},{20,8},{16,12},{12,16},{8,20},{4,24},{0,28},{29,1},{... | collective-permute-start | bytes 208904 | tf_op jit(solution)/shard_map/ppermute | solution.py:383
  81.5 1.7 %collective-permute-start.33 = (bf16[256,128]{1,0:T(8,128)(2,1)S(1)}, bf16[256,128]{1,0:T(8,128)(2,1)S(1)}, u32[]{:S(2)}, u32[]{:S(2)}) collective-permute-start(bf16[256,128]{1,0:T(8,128)(2,1)S(1)} %get-tuple-element.91.refs_0_), channel_id=1, source_target_pairs={{8,0},{12,4},{0,8},{4,12},{24,16},{28,20},{16,24},{20,28},{9,1},{1... | collective-permute-start | bytes 196616 | tf_op jit(solution)/shard_map/ppermute | solution.py:383
  84.3 1.7 %collective-permute-start.35 = (bf16[256,128]{1,0:T(8,128)(2,1)S(1)}, bf16[256,128]{1,0:T(8,128)(2,1)S(1)}, u32[]{:S(2)}, u32[]{:S(2)}) collective-permute-start(bf16[256,128]{1,0:T(8,128)(2,1)S(1)} %get-tuple-element.91.refs_0_), channel_id=1, source_target_pairs={{24,0},{28,4},{16,8},{20,12},{8,16},{12,20},{0,24},{4,28},{25,1},{... | collective-permute-start | bytes 196616 | tf_op jit(solution)/shard_map/ppermute | solution.py:383
  87.5 1.8 %collective-permute-start.36 = (bf16[256,128]{1,0:T(8,128)(2,1)S(1)}, bf16[256,128]{1,0:T(8,128)(2,1)S(1)}, u32[]{:S(2)}, u32[]{:S(2)}) collective-permute-start(bf16[256,128]{1,0:T(8,128)(2,1)S(1)} %get-tuple-element.91.refs_0_), channel_id=1, source_target_pairs={{4,0},{0,4},{12,8},{8,12},{20,16},{16,20},{28,24},{24,28},{5,1},{1... | collective-permute-start | bytes 196616 | tf_op jit(solution)/shard_map/ppermute | solution.py:383
  89.6 1.8 %collective-permute-start.38 = (bf16[256,128]{1,0:T(8,128)(2,1)S(1)}, bf16[256,128]{1,0:T(8,128)(2,1)S(1)}, u32[]{:S(2)}, u32[]{:S(2)}) collective-permute-start(bf16[256,128]{1,0:T(8,128)(2,1)S(1)} %collective-permute-done.34.refs_2_), channel_id=1, source_target_pairs={{4,0},{0,4},{12,8},{8,12},{20,16},{16,20},{28,24},{24,28},{5,1},{1... | collective-permute-start | bytes 196616 | tf_op jit(solution)/shard_map/ppermute | solution.py:383
  91.7 6.9 %shard_map.140 = (f32[1,256,512]{2,1,0:T(8,128)}, f32[1,256,512]{2,1,0:T(8,128)}, f32[1,512,256]{2,1,0:T(8,128)}) custom-call(f32[256,512]{1,0:T(8,128)S(1)} %get-tuple-element.92.refs_0_, f32[256,512]{1,0:T(8,128)S(1)} %get-tuple-element.93.refs_1_, f32[256,512]{1,0:T(8,128)S(1)} %get-tuple-element.94.refs_2_, f32[256,512]{1,0:T(8,128)S(1)} %get-tuple-element.101.refs_3_, ...), custom_call_target="tpu_custom_call" | custom-call | flops 5033164800 | bytes 4980736 | tf_op jit(solution)/shard_map/pallas_call | solution.py:129
  (89 shorter events, 36.1 us)
Async XLA Ops:
  1.9 9.3 %collective-permute-start = (bf16[256,512]{1,0:T(8,128)(2,1)S(1)}, bf16[256,512]{1,0:T(8,128)(2,1)S(1)}, u32[]{:S(2)}, u32[]{:S(2)}) collective-permute-start(bf16[256,512]{1,0:T(8,128)(2,1)S(1)} %get-tuple-element.72.refs_3_.own_ref), channel_id=1, source_target_pairs={{0,8},{8,16},{16,24},{24,28},{28,20},{20,12},{12,4},{4,0},{1,9},{9... | collective-permute-start | bytes 786440 | tf_op jit(solution)/shard_map/ppermute | solution.py:375
  5.0 8.0 %collective-permute-start.2 = (bf16[256,512]{1,0:T(8,128)(2,1)S(1)}, bf16[256,512]{1,0:T(8,128)(2,1)S(1)}, u32[]{:S(2)}, u32[]{:S(2)}) collective-permute-start(bf16[256,512]{1,0:T(8,128)(2,1)S(1)} %get-tuple-element.72.refs_3_.own_ref), channel_id=1, source_target_pairs={{8,0},{16,8},{24,16},{28,24},{20,28},{12,20},{4,12},{0,4},{9,1},{1... | collective-permute-start | bytes 786440 | tf_op jit(solution)/shard_map/ppermute | solution.py:376
  11.2 7.5 %collective-permute-start.1 = (bf16[256,512]{1,0:T(8,128)(2,1)S(1)}, bf16[256,512]{1,0:T(8,128)(2,1)S(1)}, u32[]{:S(2)}, u32[]{:S(2)}) collective-permute-start(bf16[256,512]{1,0:T(8,128)(2,1)S(1)} %collective-permute-done.refs_4_.refs_0_), channel_id=1, source_target_pairs={{0,8},{8,16},{16,24},{24,28},{28,20},{20,12},{12,4},{4,0},{1,9},{9... | collective-permute-start | bytes 786440 | tf_op jit(solution)/shard_map/ppermute | solution.py:375
  13.0 7.2 %collective-permute-start.4 = (bf16[256,512]{1,0:T(8,128)(2,1)S(1)}, bf16[256,512]{1,0:T(8,128)(2,1)S(1)}, u32[]{:S(2)}, u32[]{:S(2)}) collective-permute-start(bf16[256,512]{1,0:T(8,128)(2,1)S(1)} %collective-permute-done.2.refs_5_.refs_1_), channel_id=1, source_target_pairs={{8,0},{16,8},{24,16},{28,24},{20,28},{12,20},{4,12},{0,4},{9,1},{1... | collective-permute-start | bytes 786440 | tf_op jit(solution)/shard_map/ppermute | solution.py:376
  20.7 13.1 %collective-permute-start.12 = (bf16[256,1024]{1,0:T(8,128)(2,1)S(1)}, bf16[256,1024]{1,0:T(8,128)(2,1)S(1)}, u32[]{:S(2)}, u32[]{:S(2)}) collective-permute-start(bf16[256,1024]{1,0:T(8,128)(2,1)S(1)} %copy-done.3), channel_id=1, source_target_pairs={{2,0},{3,1},{0,2},{1,3},{6,4},{7,5},{4,6},{5,7},{10,8},{11,9},{8,1... | collective-permute-start | bytes 1572872 | tf_op jit(solution)/shard_map/ppermute | solution.py:383
  26.6 7.2 %collective-permute-start.15 = (bf16[256,512]{1,0:T(8,128)(2,1)S(1)}, bf16[256,512]{1,0:T(8,128)(2,1)S(1)}, u32[]{:S(2)}, u32[]{:S(2)}) collective-permute-start(bf16[256,512]{1,0:T(8,128)(2,1)S(1)} %get-tuple-element.75.own_ref.refs_3_), channel_id=1, source_target_pairs={{0,8},{8,16},{16,24},{24,28},{28,20},{20,12},{12,4},{4,0},{1,9},{9... | collective-permute-start | bytes 786440 | tf_op jit(solution)/shard_map/ppermute | solution.py:375
  33.8 15.7 %collective-permute-start.13 = (bf16[256,1024]{1,0:T(8,128)(2,1)S(1)}, bf16[256,1024]{1,0:T(8,128)(2,1)S(1)}, u32[]{:S(2)}, u32[]{:S(2)}) collective-permute-start(bf16[256,1024]{1,0:T(8,128)(2,1)S(1)} %copy-done.3), channel_id=1, source_target_pairs={{1,0},{0,1},{3,2},{2,3},{5,4},{4,5},{7,6},{6,7},{9,8},{8,9},{11,10... | collective-permute-start | bytes 1572872 | tf_op jit(solution)/shard_map/ppermute | solution.py:383
  33.9 11.9 %collective-permute-start.6 = (bf16[256,512]{1,0:T(8,128)(2,1)S(1)}, bf16[256,512]{1,0:T(8,128)(2,1)S(1)}, u32[]{:S(2)}, u32[]{:S(2)}) collective-permute-start(bf16[256,512]{1,0:T(8,128)(2,1)S(1)} %get-tuple-element.60), channel_id=1, source_target_pairs={{28,0},{0,4},{4,8},{8,12},{12,16},{16,20},{20,24},{24,28},{29,1},{... | collective-permute-start | bytes 786440 | tf_op jit(solution)/shard_map/ppermute | solution.py:397
  34.7 22.7 %collective-permute-start.14 = (bf16[256,1024]{1,0:T(8,128)(2,1)S(1)}, bf16[256,1024]{1,0:T(8,128)(2,1)S(1)}, u32[]{:S(2)}, u32[]{:S(2)}) collective-permute-start(bf16[256,1024]{1,0:T(8,128)(2,1)S(1)} %collective-permute-done.12.refs_5_), channel_id=1, source_target_pairs={{1,0},{0,1},{3,2},{2,3},{5,4},{4,5},{7,6},{6,7},{9,8},{8,9},{11,10... | collective-permute-start | bytes 1572872 | tf_op jit(solution)/shard_map/ppermute | solution.py:383
  35.1 16.9 %collective-permute-start.20 = (bf16[256,512]{1,0:T(8,128)(2,1)S(1)}, bf16[256,512]{1,0:T(8,128)(2,1)S(1)}, u32[]{:S(2)}, u32[]{:S(2)}) collective-permute-start(bf16[256,512]{1,0:T(8,128)(2,1)S(1)} %collective-permute-done.15.refs_4_), channel_id=1, source_target_pairs={{0,8},{8,16},{16,24},{24,28},{28,20},{20,12},{12,4},{4,0},{1,9},{9... | collective-permute-start | bytes 786440 | tf_op jit(solution)/shard_map/ppermute | solution.py:375
  36.8 15.7 %collective-permute-start.21 = (bf16[256,512]{1,0:T(8,128)(2,1)S(1)}, bf16[256,512]{1,0:T(8,128)(2,1)S(1)}, u32[]{:S(2)}, u32[]{:S(2)}) collective-permute-start(bf16[256,512]{1,0:T(8,128)(2,1)S(1)} %collective-permute-done.16.refs_5_), channel_id=1, source_target_pairs={{8,0},{16,8},{24,16},{28,24},{20,28},{12,20},{4,12},{0,4},{9,1},{1... | collective-permute-start | bytes 786440 | tf_op jit(solution)/shard_map/ppermute | solution.py:376
  52.5 8.3 %collective-permute-start.22 = (bf16[256,512]{1,0:T(8,128)(2,1)S(1)}, bf16[256,512]{1,0:T(8,128)(2,1)S(1)}, u32[]{:S(2)}, u32[]{:S(2)}) collective-permute-start(bf16[256,512]{1,0:T(8,128)(2,1)S(1)} %collective-permute-done.20.refs_3_), channel_id=1, source_target_pairs={{0,8},{8,16},{16,24},{24,28},{28,20},{20,12},{12,4},{4,0},{1,9},{9... | collective-permute-start | bytes 786440 | tf_op jit(solution)/shard_map/ppermute | solution.py:375
  54.6 8.6 %collective-permute-start.18 = (bf16[256,256]{1,0:T(8,128)(2,1)S(1)}, bf16[256,256]{1,0:T(8,128)(2,1)S(1)}, u32[]{:S(2)}, u32[]{:S(2)}) collective-permute-start(bf16[256,256]{1,0:T(8,128)(2,1)S(1)} %shard_map.131.refs_0_), channel_id=1, source_target_pairs={{1,0},{0,1},{3,2},{2,3},{5,4},{4,5},{7,6},{6,7},{9,8},{8,9},{11,10... | collective-permute-start | bytes 393224 | tf_op jit(solution)/shard_map/ppermute | solution.py:383
  60.8 11.7 %collective-permute-start.23 = (bf16[128,512]{1,0:T(8,128)(2,1)S(1)}, bf16[128,512]{1,0:T(8,128)(2,1)S(1)}, u32[]{:S(2)}, u32[]{:S(2)}) collective-permute-start(bf16[128,512]{1,0:T(8,128)(2,1)S(1)} %slice.36), channel_id=1, source_target_pairs={{0,8},{8,16},{16,24},{24,28},{28,20},{20,12},{12,4},{4,0},{1,9},{9... | collective-permute-start | bytes 393224 | tf_op jit(solution)/shard_map/ppermute | solution.py:371
  61.2 13.0 %collective-permute-start.25 = (bf16[128,512]{1,0:T(8,128)(2,1)S(1)}, bf16[128,512]{1,0:T(8,128)(2,1)S(1)}, u32[]{:S(2)}, u32[]{:S(2)}) collective-permute-start(bf16[128,512]{1,0:T(8,128)(2,1)S(1)} %slice.37), channel_id=1, source_target_pairs={{8,0},{16,8},{24,16},{28,24},{20,28},{12,20},{4,12},{0,4},{9,1},{1... | collective-permute-start | bytes 393224 | tf_op jit(solution)/shard_map/ppermute | solution.py:372
  66.0 12.6 %collective-permute-start.28 = (bf16[272,128]{1,0:T(8,128)(2,1)S(1)}, bf16[272,128]{1,0:T(8,128)(2,1)S(1)}, u32[]{:S(2)}, u32[]{:S(2)}) collective-permute-start(bf16[272,128]{1,0:T(8,128)(2,1)S(1)} %get-tuple-element.86), channel_id=1, source_target_pairs={{12,0},{8,4},{4,8},{0,12},{28,16},{24,20},{20,24},{16,28},{13,1},{... | collective-permute-start | bytes 208904 | tf_op jit(solution)/shard_map/ppermute | solution.py:383
  69.4 9.2 %collective-permute-start.29 = (bf16[272,128]{1,0:T(8,128)(2,1)S(1)}, bf16[272,128]{1,0:T(8,128)(2,1)S(1)}, u32[]{:S(2)}, u32[]{:S(2)}) collective-permute-start(bf16[272,128]{1,0:T(8,128)(2,1)S(1)} %get-tuple-element.87), channel_id=1, source_target_pairs={{16,0},{20,4},{24,8},{28,12},{0,16},{4,20},{8,24},{12,28},{17,1},{... | collective-permute-start | bytes 208904 | tf_op jit(solution)/shard_map/ppermute | solution.py:383
  70.1 10.0 %collective-permute-start.30 = (bf16[272,128]{1,0:T(8,128)(2,1)S(1)}, bf16[272,128]{1,0:T(8,128)(2,1)S(1)}, u32[]{:S(2)}, u32[]{:S(2)}) collective-permute-start(bf16[272,128]{1,0:T(8,128)(2,1)S(1)} %get-tuple-element.88), channel_id=1, source_target_pairs={{20,0},{16,4},{28,8},{24,12},{4,16},{0,20},{12,24},{8,28},{21,1},{... | collective-permute-start | bytes 208904 | tf_op jit(solution)/shard_map/ppermute | solution.py:383
  72.5 7.6 %collective-permute-start.31 = (bf16[272,128]{1,0:T(8,128)(2,1)S(1)}, bf16[272,128]{1,0:T(8,128)(2,1)S(1)}, u32[]{:S(2)}, u32[]{:S(2)}) collective-permute-start(bf16[272,128]{1,0:T(8,128)(2,1)S(1)} %get-tuple-element.89), channel_id=1, source_target_pairs={{24,0},{28,4},{16,8},{20,12},{8,16},{12,20},{0,24},{4,28},{25,1},{... | collective-permute-start | bytes 208904 | tf_op jit(solution)/shard_map/ppermute | solution.py:383
  81.5 7.8 %collective-permute-start.33 = (bf16[256,128]{1,0:T(8,128)(2,1)S(1)}, bf16[256,128]{1,0:T(8,128)(2,1)S(1)}, u32[]{:S(2)}, u32[]{:S(2)}) collective-permute-start(bf16[256,128]{1,0:T(8,128)(2,1)S(1)} %get-tuple-element.91.refs_0_), channel_id=1, source_target_pairs={{8,0},{12,4},{0,8},{4,12},{24,16},{28,20},{16,24},{20,28},{9,1},{1... | collective-permute-start | bytes 196616 | tf_op jit(solution)/shard_map/ppermute | solution.py:383
  87.5 11.6 %collective-permute-start.36 = (bf16[256,128]{1,0:T(8,128)(2,1)S(1)}, bf16[256,128]{1,0:T(8,128)(2,1)S(1)}, u32[]{:S(2)}, u32[]{:S(2)}) collective-permute-start(bf16[256,128]{1,0:T(8,128)(2,1)S(1)} %get-tuple-element.91.refs_0_), channel_id=1, source_target_pairs={{4,0},{0,4},{12,8},{8,12},{20,16},{16,20},{28,24},{24,28},{5,1},{1... | collective-permute-start | bytes 196616 | tf_op jit(solution)/shard_map/ppermute | solution.py:383
  89.3 9.8 %collective-permute-start.37 = (bf16[256,128]{1,0:T(8,128)(2,1)S(1)}, bf16[256,128]{1,0:T(8,128)(2,1)S(1)}, u32[]{:S(2)}, u32[]{:S(2)}) collective-permute-start(bf16[256,128]{1,0:T(8,128)(2,1)S(1)} %collective-permute-done.33.refs_1_), channel_id=1, source_target_pairs={{4,0},{0,4},{12,8},{8,12},{20,16},{16,20},{28,24},{24,28},{5,1},{1... | collective-permute-start | bytes 196616 | tf_op jit(solution)/shard_map/ppermute | solution.py:383
  89.6 9.5 %collective-permute-start.38 = (bf16[256,128]{1,0:T(8,128)(2,1)S(1)}, bf16[256,128]{1,0:T(8,128)(2,1)S(1)}, u32[]{:S(2)}, u32[]{:S(2)}) collective-permute-start(bf16[256,128]{1,0:T(8,128)(2,1)S(1)} %collective-permute-done.34.refs_2_), channel_id=1, source_target_pairs={{4,0},{0,4},{12,8},{8,12},{20,16},{16,20},{28,24},{24,28},{5,1},{1... | collective-permute-start | bytes 196616 | tf_op jit(solution)/shard_map/ppermute | solution.py:383
  91.3 7.8 %collective-permute-start.39 = (bf16[256,128]{1,0:T(8,128)(2,1)S(1)}, bf16[256,128]{1,0:T(8,128)(2,1)S(1)}, u32[]{:S(2)}, u32[]{:S(2)}) collective-permute-start(bf16[256,128]{1,0:T(8,128)(2,1)S(1)} %collective-permute-done.35.refs_3_), channel_id=1, source_target_pairs={{4,0},{0,4},{12,8},{8,12},{20,16},{16,20},{28,24},{24,28},{5,1},{1... | collective-permute-start | bytes 196616 | tf_op jit(solution)/shard_map/ppermute | solution.py:383
  (21 other events, 124.2 us)

commit v3 on v2

--- a/solution.py
+++ b/solution.py
@@ -70,24 +70,17 @@
             halves = [g.astype(BF16) for g in grams]
             polys = [(b * g + c * mm(h, h)).astype(BF16) for g, h in zip(grams, halves)]
             xs = [a * x + mm(p, low) for x, p, low in zip(xs, polys, lows)]
-        elif sweep == 2:
-            pairs = [split(x) for x in xs]
-            grams = [mm_nt(h, h) + mm_nt(h, l) + mm_nt(l, h) for h, l in pairs]
-            gpairs = [split(g) for g in grams]
-            polys = [
-                b * g + c * (mm(h, h) + mm(h, l) + mm(l, h)) for g, (h, l) in zip(grams, gpairs)
-            ]
-            ppairs = [split(p) for p in polys]
-            xs = [
-                a * x + (mm(ph, h) + mm(ph, l) + mm(pl_, h))
-                for x, (ph, pl_), (h, l) in zip(xs, ppairs, pairs)
-            ]
         else:
             lows = [x.astype(BF16) for x in xs]
             grams = [mm_nt(x, x) for x in lows]
-            moved = [jnp.where(diag, g - centre, g).astype(BF16) for g in grams]
-            polys = [(c * mm(h, h)).astype(BF16) for h in moved]
-            xs = [rest * x + mm(p, low) for x, p, low in zip(xs, polys, lows)]
+            moved = [jnp.where(diag, g - centre, g) for g in grams]
+            if sweep == 2:
+                pairs = [split(m) for m in moved]
+                polys = [split(c * (mm(h, h) + mm(h, l) + mm(l, h))) for h, l in pairs]
+            else:
+                halves = [m.astype(BF16) for m in moved]
+                polys = [((c * mm(h, h)).astype(BF16),) for h in halves]
+            xs = [rest * x + sum(mm(p, low) for p in poly) for x, poly, low in zip(xs, polys, lows)]
     return xs
 
 
@@ -123,14 +116,15 @@
     )
 
 
-def call(kernel, outs, args, flops=0, scratch=()):
+def call(kernel, outs, args, flops=0, scratch=(), scalars=0):
     vmem = pl.BlockSpec(memory_space=pltpu.VMEM)
+    smem = pl.BlockSpec(memory_space=pltpu.SMEM)
     size = sum(math.prod(a.shape) * a.dtype.itemsize for a in list(args) + list(outs))
     return pl.pallas_call(
         kernel,
         out_shape=tuple(jax.ShapeDtypeStruct(o.shape, o.dtype) for o in outs),
         in_specs=[vmem] * len(args),
-        out_specs=tuple([vmem] * len(outs)),
+        out_specs=tuple([vmem] * (len(outs) - scalars) + [smem] * scalars),
         scratch_shapes=list(scratch),
         compiler_params=pltpu.CompilerParams(vmem_limit_bytes=VMEM_BYTES),
         cost_estimate=pl.CostEstimate(flops=flops, bytes_accessed=size, transcendentals=0),
@@ -292,7 +286,7 @@
 
             term_ref[...] = part(place)
             for offset, send in enumerate(outs[3:-2], start=1):
-                send[:width, :] = part(place ^ offset).astype(BF16)
+                send[:width, :] = part(lax.rem(place + offset, chunks)).astype(BF16)
                 for at in range(0, chunk, LANES):
                     send[width:, at : at + LANES] = tile
 
@@ -312,19 +306,28 @@
 
 def outer_total(own, loss, gots, grad_scale, loss_scale):
     width, chunk = own.shape
+    seq = len(gots) + 1
 
     def kernel(own_ref, loss_ref, *rest):
         got_refs, out_ref, new_loss_ref = rest[:-2], rest[-2], rest[-1]
+        me = lax.axis_index("seq")
         total = own_ref[...]
-        sq = jnp.max(loss_ref[...])
-        for got in got_refs:
+        lane = lax.broadcasted_iota(jnp.int32, (LOSS_ROWS, LANES), 1)
+        own_tile = loss_tile(jnp.max(loss_ref[...]))
+        spread = jnp.where(lane == me, own_tile.astype(F32), 0.0)
+        for offset, got in enumerate(got_refs, start=1):
             total = total + got[:width, :].astype(F32)
-            sq = sq + tile_loss(got[width:, :LANES])
+            here = lane == lax.rem(me + seq - offset, seq)
+            spread = spread + jnp.where(here, got[width:, :LANES].astype(F32), 0.0)
+        loss = jnp.sum(spread) * (2.0 / LOSS_ROWS)
         out_ref[...] = (total * grad_scale).astype(BF16)
-        new_loss_ref[...] = jnp.full((8, LANES), sq * loss_scale, F32)
+        new_loss_ref[0, 0] = loss * loss_scale
 
     return call(
-        kernel, [like((width, chunk), BF16), like((8, LANES), F32)], [own, loss] + list(gots)
+        kernel,
+        [like((width, chunk), BF16), like((1, 1), F32)],
+        [own, loss] + list(gots),
+        scalars=1,
     )
 
 
@@ -381,6 +384,16 @@
 def partner(block, axis, bit):
     size = lax.axis_size(axis)
     return lax.ppermute(block, axis, [(i ^ bit, i) for i in range(size)])
+
+
+def shifted(blocks, axis):
+    size = lax.axis_size(axis)
+    got = [None] * len(blocks)
+    for far in range(size // 2, 0, -1):
+        for shift in dict.fromkeys((far, size - far)):
+            pairs = [(d, (d + shift) % size) for d in range(size)]
+            got[shift - 1] = lax.ppermute(blocks[shift - 1], axis, pairs)
+    return got
 
 
 def cube_gather(block, axis):
@@ -489,14 +502,14 @@
     new_first, new_third, new_second = update(weights, grads, final)
 
     if chunks:
-        gots = [partner(s, "seq", m) for m, s in enumerate(sends, start=1)]
+        gots = shifted(sends, "seq")
         term = after(term, *final)
         piece, loss = outer_total(term, loss, gots, grad_scale, loss_scale)
         line = [(2 * m, partner(piece, "seq", 2 * m)) for m in range(1, seq // 2)]
         pieces = [(0, piece)] + line
         pieces += [(m + 1, partner(p, "seq", 1)) for m, p in pieces]
         out_grad = assemble([p for _, p in pieces], [m for m, _ in pieces], cols)
-        distill_loss = loss[0, 0]
+        distill_loss = loss.reshape(())
     else:
         term, loss = lax.psum((term, loss), "seq")
         out_grad = term * grad_scale

time: 100 us -> 99.1 us (level)
    ppermute x23 -> x16, starting transfers between devices: 24.5 us -> 14.6 us  [partner(): return lax.ppermute(block, axis, [(i ^ bit, i) for i in range(size)])]
    ppermute x0 -> x7, starting transfers between devices: none -> 9.43 us  [shifted(): got[shift - 1] = lax.ppermute(blocks[shift - 1], axis, pairs)]
    ppermute x0 -> x7, waiting for transfers between devices: none -> 3.5 us  [shifted(): got[shift - 1] = lax.ppermute(blocks[shift - 1], axis, pairs)]
    ppermute x23 -> x16, waiting for transfers between devices: 7.35 us -> 3.96 us  [partner(): return lax.ppermute(block, axis, [(i ^ bit, i) for i in range(size)])]
  transfers between devices with their start and end apart: 40 -> 40, of which waited for: 14 -> 13; matrix products, arithmetic and copies ran while one was open for 3% -> 2% of each run, Pallas kernels for 28% -> 27%
where the time goes in v3:
time: 99.1 us; the launch traced here: 99 us
  starting transfers between devices  40.2 us (41%)
  Pallas kernels  28.9 us (29%)
  waiting for transfers between devices  25.7 us (26%)
  local copies, waits for them, and re-layouts  2.43 us (2%)
    pallas_call x14, Pallas kernels, call(): pl.pallas_call(kernel, out_shape=tuple((jax.ShapeDtypeStruct(o.shape, o.d...  28.9 us
    ppermute x16, starting transfers between devices, partner(): return lax.ppermute(block, axis, [(i ^ bit, i) for i in range(size)])  14.6 us
    ppermute x6, waiting for transfers between devices, step(): self.up = lax.ppermute(up, self.axis, self.ahead)  13.6 us
    ppermute x6, starting transfers between devices, step(): self.up = lax.ppermute(up, self.axis, self.ahead)  9.51 us
    ppermute x7, starting transfers between devices, shifted(): got[shift - 1] = lax.ppermute(blocks[shift - 1], axis, pairs)  9.43 us
    ppermute x16, waiting for transfers between devices, partner(): return lax.ppermute(block, axis, [(i ^ bit, i) for i in range(size)])  3.96 us
    ppermute x7, waiting for transfers between devices, shifted(): got[shift - 1] = lax.ppermute(blocks[shift - 1], axis, pairs)  3.5 us
    ppermute x1, waiting for transfers between devices, from_behind(): return lax.ppermute(block, axis, [((i - 1) % size, i) for i in range(size)])  2.6 us
  transfers between devices with their start and end apart: 40, of which 13 were waited for; matrix products, arithmetic and copies ran while one was open for 2% of the time, Pallas kernels for 27%

profile of v3, /device:TPU:0, one launch (start us, length us, event | category | flops | bytes accessed | tf_op | source)
XLA Modules:
  0.0 99.0 jit_solution(9062707975571610258)
XLA Ops:
  1.9 3.1 %collective-permute-start = (bf16[256,512]{1,0:T(8,128)(2,1)S(1)}, bf16[256,512]{1,0:T(8,128)(2,1)S(1)}, u32[]{:S(2)}, u32[]{:S(2)}) collective-permute-start(bf16[256,512]{1,0:T(8,128)(2,1)S(1)} %get-tuple-element.72.refs_3_.own_ref), channel_id=1, source_target_pairs={{0,8},{8,16},{16,24},{24,28},{28,20},{20,12},{12,4},{4,0},{1,9},{9... | collective-permute-start | bytes 786440 | tf_op jit(solution)/shard_map/ppermute | solution.py:378
  5.0 6.2 %collective-permute-done.refs_4_.refs_0_ = bf16[256,512]{1,0:T(8,128)(2,1)S(1)} collective-permute-done((bf16[256,512]{1,0:T(8,128)(2,1)S(1)}, bf16[256,512]{1,0:T(8,128)(2,1)S(1)}, u32[]{:S(2)}, u32[]{:S(2)}) %collective-permute-start) | collective-permute-done | bytes 262176 | tf_op jit(solution)/shard_map/ppermute | solution.py:378
  11.2 1.8 %collective-permute-start.1 = (bf16[256,512]{1,0:T(8,128)(2,1)S(1)}, bf16[256,512]{1,0:T(8,128)(2,1)S(1)}, u32[]{:S(2)}, u32[]{:S(2)}) collective-permute-start(bf16[256,512]{1,0:T(8,128)(2,1)S(1)} %collective-permute-done.refs_4_.refs_0_), channel_id=1, source_target_pairs={{0,8},{8,16},{16,24},{24,28},{28,20},{20,12},{12,4},{4,0},{1,9},{9... | collective-permute-start | bytes 786440 | tf_op jit(solution)/shard_map/ppermute | solution.py:378
  14.5 2.2 %shard_map.127 = (f32[256,512]{1,0:T(8,128)S(1)}, f32[256,512]{1,0:T(8,128)S(1)}, f32[256,512]{1,0:T(8,128)S(1)}) custom-call(f32[256,512]{1,0:T(8,128)S(1)} %bitcast.21, f32[256,512]{1,0:T(8,128)S(1)} %bitcast.26, f32[256,512]{1,0:T(8,128)S(1)} %bitcast.16, bf16[256,512]{1,0:T(8,128)(2,1)S(1)} %get-tuple-element.72.refs_3_.own_ref, ...), custom_call_target="tpu_custom_call" | custom-call | flops 1207959552 | bytes 3932160 | tf_op jit(solution)/shard_map/pallas_call | solution.py:123
  16.8 1.9 %collective-permute-done.1.refs_3_.refs_2_ = bf16[256,512]{1,0:T(8,128)(2,1)S(1)} collective-permute-done((bf16[256,512]{1,0:T(8,128)(2,1)S(1)}, bf16[256,512]{1,0:T(8,128)(2,1)S(1)}, u32[]{:S(2)}, u32[]{:S(2)}) %collective-permute-start.1) | collective-permute-done | bytes 262176 | tf_op jit(solution)/shard_map/ppermute | solution.py:378
  22.1 3.1 %collective-permute-done.3.refs_3_.refs_4_ = bf16[256,512]{1,0:T(8,128)(2,1)S(1)} collective-permute-done((bf16[256,512]{1,0:T(8,128)(2,1)S(1)}, bf16[256,512]{1,0:T(8,128)(2,1)S(1)}, u32[]{:S(2)}, u32[]{:S(2)}) %collective-permute-start.3) | collective-permute-done | bytes 262176 | tf_op jit(solution)/shard_map/ppermute | solution.py:378
  30.1 1.6 %collective-permute-start.7 = (bf16[128,512]{1,0:T(8,128)(2,1)S(1)}, bf16[128,512]{1,0:T(8,128)(2,1)S(1)}, u32[]{:S(2)}, u32[]{:S(2)}) collective-permute-start(bf16[128,512]{1,0:T(8,128)(2,1)S(1)} %slice.28), channel_id=1, source_target_pairs={{0,8},{8,16},{16,24},{24,28},{28,20},{20,12},{12,4},{4,0},{1,9},{9... | collective-permute-start | bytes 393224 | tf_op jit(solution)/shard_map/ppermute | solution.py:374
  35.1 1.6 %collective-permute-start.20 = (bf16[256,512]{1,0:T(8,128)(2,1)S(1)}, bf16[256,512]{1,0:T(8,128)(2,1)S(1)}, u32[]{:S(2)}, u32[]{:S(2)}) collective-permute-start(bf16[256,512]{1,0:T(8,128)(2,1)S(1)} %collective-permute-done.15.refs_4_), channel_id=1, source_target_pairs={{0,8},{8,16},{16,24},{24,28},{28,20},{20,12},{12,4},{4,0},{1,9},{9... | collective-permute-start | bytes 786440 | tf_op jit(solution)/shard_map/ppermute | solution.py:378
  37.4 5.8 %shard_map.130 = (f32[256,512]{1,0:T(8,128)S(1)}, f32[256,512]{1,0:T(8,128)S(1)}, f32[256,512]{1,0:T(8,128)S(1)}, f32[256,256]{1,0:T(8,128)S(1)}) custom-call(f32[256,512]{1,0:T(8,128)S(1)} %bitcast.24, f32[256,512]{1,0:T(8,128)S(1)} %bitcast.29, f32[256,512]{1,0:T(8,128)S(1)} %bitcast.19, f32[256,512]{1,0:T(8,128)S(1)} %get-tuple-element.66.refs_3_, ...), custom_call_target="tpu_custom_call" | custom-call | flops 5033164800 | bytes 5505024 | tf_op jit(solution)/shard_map/pallas_call | solution.py:123
  43.2 2.6 %collective-permute-done.6.behind_ref = bf16[256,512]{1,0:T(8,128)(2,1)S(1)} collective-permute-done((bf16[256,512]{1,0:T(8,128)(2,1)S(1)}, bf16[256,512]{1,0:T(8,128)(2,1)S(1)}, u32[]{:S(2)}, u32[]{:S(2)}) %collective-permute-start.6) | collective-permute-done | bytes 262176 | tf_op jit(solution)/shard_map/ppermute | solution.py:410
  50.1 1.9 %collective-permute-done.17.refs_1_ = bf16[256,256]{1,0:T(8,128)(2,1)S(1)} collective-permute-done((bf16[256,256]{1,0:T(8,128)(2,1)S(1)}, bf16[256,256]{1,0:T(8,128)(2,1)S(1)}, u32[]{:S(2)}, u32[]{:S(2)}) %collective-permute-start.17) | collective-permute-done | bytes 131104 | tf_op jit(solution)/shard_map/ppermute | solution.py:386
  52.5 2.0 %collective-permute-done.9.refs_1_ = bf16[256,256]{1,0:T(8,128)(2,1)S(1)} collective-permute-done((bf16[256,256]{1,0:T(8,128)(2,1)S(1)}, bf16[256,256]{1,0:T(8,128)(2,1)S(1)}, u32[]{:S(2)}, u32[]{:S(2)}) %collective-permute-start.9) | collective-permute-done | bytes 131104 | tf_op jit(solution)/shard_map/ppermute | solution.py:386
  55.1 2.3 %shard_map.137 = (f32[256,512]{1,0:T(8,128)S(1)}, f32[256,512]{1,0:T(8,128)S(1)}, f32[256,512]{1,0:T(8,128)S(1)}) custom-call(f32[256,512]{1,0:T(8,128)S(1)} %get-tuple-element.92.refs_0_, f32[256,512]{1,0:T(8,128)S(1)} %get-tuple-element.93.refs_1_, f32[256,512]{1,0:T(8,128)S(1)} %get-tuple-element.94.refs_2_, ...), custom_call_target="tpu_custom_call" | custom-call | flops 1207959552 | bytes 3932160 | tf_op jit(solution)/shard_map/pallas_call | solution.py:123
  58.5 2.3 %collective-permute-done.22.refs_3_ = bf16[256,512]{1,0:T(8,128)(2,1)S(1)} collective-permute-done((bf16[256,512]{1,0:T(8,128)(2,1)S(1)}, bf16[256,512]{1,0:T(8,128)(2,1)S(1)}, u32[]{:S(2)}, u32[]{:S(2)}) %collective-permute-start.22) | collective-permute-done | bytes 262176 | tf_op jit(solution)/shard_map/ppermute | solution.py:378
  61.2 1.8 %collective-permute-start.25 = (bf16[128,512]{1,0:T(8,128)(2,1)S(1)}, bf16[128,512]{1,0:T(8,128)(2,1)S(1)}, u32[]{:S(2)}, u32[]{:S(2)}) collective-permute-start(bf16[128,512]{1,0:T(8,128)(2,1)S(1)} %slice.33), channel_id=1, source_target_pairs={{8,0},{16,8},{24,16},{28,24},{20,28},{12,20},{4,12},{0,4},{9,1},{1... | collective-permute-start | bytes 393224 | tf_op jit(solution)/shard_map/ppermute | solution.py:375
  65.1 3.2 %collective-permute-start.28 = (bf16[272,128]{1,0:T(8,128)(2,1)S(1)}, bf16[272,128]{1,0:T(8,128)(2,1)S(1)}, u32[]{:S(2)}, u32[]{:S(2)}) collective-permute-start(bf16[272,128]{1,0:T(8,128)(2,1)S(1)} %get-tuple-element.86), channel_id=1, source_target_pairs={{0,12},{4,16},{8,20},{12,24},{16,28},{20,0},{24,4},{28,8},{1,13},{... | collective-permute-start | bytes 208904 | tf_op jit(solution)/shard_map/ppermute | solution.py:395
  69.0 2.3 %collective-permute-done.26.rest_0_ = bf16[272,128]{1,0:T(8,128)(2,1)S(1)} collective-permute-done((bf16[272,128]{1,0:T(8,128)(2,1)S(1)}, bf16[272,128]{1,0:T(8,128)(2,1)S(1)}, u32[]{:S(2)}, u32[]{:S(2)}) %collective-permute-start.26) | collective-permute-done | bytes 69664 | tf_op jit(solution)/shard_map/ppermute | solution.py:395
  71.2 3.1 %collective-permute-start.30 = (bf16[272,128]{1,0:T(8,128)(2,1)S(1)}, bf16[272,128]{1,0:T(8,128)(2,1)S(1)}, u32[]{:S(2)}, u32[]{:S(2)}) collective-permute-start(bf16[272,128]{1,0:T(8,128)(2,1)S(1)} %get-tuple-element.88), channel_id=1, source_target_pairs={{0,20},{4,24},{8,28},{12,0},{16,4},{20,8},{24,12},{28,16},{1,21},{... | collective-permute-start | bytes 208904 | tf_op jit(solution)/shard_map/ppermute | solution.py:395
  74.6 2.0 %collective-permute-start.32 = (bf16[272,128]{1,0:T(8,128)(2,1)S(1)}, bf16[272,128]{1,0:T(8,128)(2,1)S(1)}, u32[]{:S(2)}, u32[]{:S(2)}) collective-permute-start(bf16[272,128]{1,0:T(8,128)(2,1)S(1)} %get-tuple-element.90), channel_id=1, source_target_pairs={{0,28},{4,0},{8,4},{12,8},{16,12},{20,16},{24,20},{28,24},{1,29},{... | collective-permute-start | bytes 208904 | tf_op jit(solution)/shard_map/ppermute | solution.py:395
  80.2 1.7 %collective-permute-start.33 = (bf16[256,128]{1,0:T(8,128)(2,1)S(1)}, bf16[256,128]{1,0:T(8,128)(2,1)S(1)}, u32[]{:S(2)}, u32[]{:S(2)}) collective-permute-start(bf16[256,128]{1,0:T(8,128)(2,1)S(1)} %get-tuple-element.91.refs_0_), channel_id=1, source_target_pairs={{8,0},{12,4},{0,8},{4,12},{24,16},{28,20},{16,24},{20,28},{9,1},{1... | collective-permute-start | bytes 196616 | tf_op jit(solution)/shard_map/ppermute | solution.py:386
  82.8 1.9 %collective-permute-start.35 = (bf16[256,128]{1,0:T(8,128)(2,1)S(1)}, bf16[256,128]{1,0:T(8,128)(2,1)S(1)}, u32[]{:S(2)}, u32[]{:S(2)}) collective-permute-start(bf16[256,128]{1,0:T(8,128)(2,1)S(1)} %get-tuple-element.91.refs_0_), channel_id=1, source_target_pairs={{24,0},{28,4},{16,8},{20,12},{8,16},{12,20},{0,24},{4,28},{25,1},{... | collective-permute-start | bytes 196616 | tf_op jit(solution)/shard_map/ppermute | solution.py:386
  86.1 3.0 %collective-permute-start.36 = (bf16[256,128]{1,0:T(8,128)(2,1)S(1)}, bf16[256,128]{1,0:T(8,128)(2,1)S(1)}, u32[]{:S(2)}, u32[]{:S(2)}) collective-permute-start(bf16[256,128]{1,0:T(8,128)(2,1)S(1)} %get-tuple-element.91.refs_0_), channel_id=1, source_target_pairs={{4,0},{0,4},{12,8},{8,12},{20,16},{16,20},{28,24},{24,28},{5,1},{1... | collective-permute-start | bytes 196616 | tf_op jit(solution)/shard_map/ppermute | solution.py:386
  89.2 1.9 %collective-permute-start.38 = (bf16[256,128]{1,0:T(8,128)(2,1)S(1)}, bf16[256,128]{1,0:T(8,128)(2,1)S(1)}, u32[]{:S(2)}, u32[]{:S(2)}) collective-permute-start(bf16[256,128]{1,0:T(8,128)(2,1)S(1)} %collective-permute-done.34.refs_2_), channel_id=1, source_target_pairs={{4,0},{0,4},{12,8},{8,12},{20,16},{16,20},{28,24},{24,28},{5,1},{1... | collective-permute-start | bytes 196616 | tf_op jit(solution)/shard_map/ppermute | solution.py:386
  91.6 6.2 %shard_map.140 = (f32[1,256,512]{2,1,0:T(8,128)}, f32[1,256,512]{2,1,0:T(8,128)}, f32[1,512,256]{2,1,0:T(8,128)}) custom-call(f32[256,512]{1,0:T(8,128)S(1)} %get-tuple-element.92.refs_0_, f32[256,512]{1,0:T(8,128)S(1)} %get-tuple-element.93.refs_1_, f32[256,512]{1,0:T(8,128)S(1)} %get-tuple-element.94.refs_2_, f32[256,512]{1,0:T(8,128)S(1)} %get-tuple-element.101.refs_3_, ...), custom_call_target="tpu_custom_call" | custom-call | flops 5033164800 | bytes 4980736 | tf_op jit(solution)/shard_map/pallas_call | solution.py:123
  (88 shorter events, 32.5 us)
Async XLA Ops:
  1.9 9.3 %collective-permute-start = (bf16[256,512]{1,0:T(8,128)(2,1)S(1)}, bf16[256,512]{1,0:T(8,128)(2,1)S(1)}, u32[]{:S(2)}, u32[]{:S(2)}) collective-permute-start(bf16[256,512]{1,0:T(8,128)(2,1)S(1)} %get-tuple-element.72.refs_3_.own_ref), channel_id=1, source_target_pairs={{0,8},{8,16},{16,24},{24,28},{28,20},{20,12},{12,4},{4,0},{1,9},{9... | collective-permute-start | bytes 786440 | tf_op jit(solution)/shard_map/ppermute | solution.py:378
  5.0 8.0 %collective-permute-start.2 = (bf16[256,512]{1,0:T(8,128)(2,1)S(1)}, bf16[256,512]{1,0:T(8,128)(2,1)S(1)}, u32[]{:S(2)}, u32[]{:S(2)}) collective-permute-start(bf16[256,512]{1,0:T(8,128)(2,1)S(1)} %get-tuple-element.72.refs_3_.own_ref), channel_id=1, source_target_pairs={{8,0},{16,8},{24,16},{28,24},{20,28},{12,20},{4,12},{0,4},{9,1},{1... | collective-permute-start | bytes 786440 | tf_op jit(solution)/shard_map/ppermute | solution.py:379
  11.2 7.5 %collective-permute-start.1 = (bf16[256,512]{1,0:T(8,128)(2,1)S(1)}, bf16[256,512]{1,0:T(8,128)(2,1)S(1)}, u32[]{:S(2)}, u32[]{:S(2)}) collective-permute-start(bf16[256,512]{1,0:T(8,128)(2,1)S(1)} %collective-permute-done.refs_4_.refs_0_), channel_id=1, source_target_pairs={{0,8},{8,16},{16,24},{24,28},{28,20},{20,12},{12,4},{4,0},{1,9},{9... | collective-permute-start | bytes 786440 | tf_op jit(solution)/shard_map/ppermute | solution.py:378
  13.0 7.2 %collective-permute-start.4 = (bf16[256,512]{1,0:T(8,128)(2,1)S(1)}, bf16[256,512]{1,0:T(8,128)(2,1)S(1)}, u32[]{:S(2)}, u32[]{:S(2)}) collective-permute-start(bf16[256,512]{1,0:T(8,128)(2,1)S(1)} %collective-permute-done.2.refs_5_.refs_1_), channel_id=1, source_target_pairs={{8,0},{16,8},{24,16},{28,24},{20,28},{12,20},{4,12},{0,4},{9,1},{1... | collective-permute-start | bytes 786440 | tf_op jit(solution)/shard_map/ppermute | solution.py:379
  20.7 13.1 %collective-permute-start.12 = (bf16[256,1024]{1,0:T(8,128)(2,1)S(1)}, bf16[256,1024]{1,0:T(8,128)(2,1)S(1)}, u32[]{:S(2)}, u32[]{:S(2)}) collective-permute-start(bf16[256,1024]{1,0:T(8,128)(2,1)S(1)} %copy-done.3), channel_id=1, source_target_pairs={{2,0},{3,1},{0,2},{1,3},{6,4},{7,5},{4,6},{5,7},{10,8},{11,9},{8,1... | collective-permute-start | bytes 1572872 | tf_op jit(solution)/shard_map/ppermute | solution.py:386
  26.6 7.2 %collective-permute-start.15 = (bf16[256,512]{1,0:T(8,128)(2,1)S(1)}, bf16[256,512]{1,0:T(8,128)(2,1)S(1)}, u32[]{:S(2)}, u32[]{:S(2)}) collective-permute-start(bf16[256,512]{1,0:T(8,128)(2,1)S(1)} %get-tuple-element.75.own_ref.refs_3_), channel_id=1, source_target_pairs={{0,8},{8,16},{16,24},{24,28},{28,20},{20,12},{12,4},{4,0},{1,9},{9... | collective-permute-start | bytes 786440 | tf_op jit(solution)/shard_map/ppermute | solution.py:378
  33.8 15.7 %collective-permute-start.13 = (bf16[256,1024]{1,0:T(8,128)(2,1)S(1)}, bf16[256,1024]{1,0:T(8,128)(2,1)S(1)}, u32[]{:S(2)}, u32[]{:S(2)}) collective-permute-start(bf16[256,1024]{1,0:T(8,128)(2,1)S(1)} %copy-done.3), channel_id=1, source_target_pairs={{1,0},{0,1},{3,2},{2,3},{5,4},{4,5},{7,6},{6,7},{9,8},{8,9},{11,10... | collective-permute-start | bytes 1572872 | tf_op jit(solution)/shard_map/ppermute | solution.py:386
  33.9 11.9 %collective-permute-start.6 = (bf16[256,512]{1,0:T(8,128)(2,1)S(1)}, bf16[256,512]{1,0:T(8,128)(2,1)S(1)}, u32[]{:S(2)}, u32[]{:S(2)}) collective-permute-start(bf16[256,512]{1,0:T(8,128)(2,1)S(1)} %get-tuple-element.60), channel_id=1, source_target_pairs={{28,0},{0,4},{4,8},{8,12},{12,16},{16,20},{20,24},{24,28},{29,1},{... | collective-permute-start | bytes 786440 | tf_op jit(solution)/shard_map/ppermute | solution.py:410
  34.7 22.7 %collective-permute-start.14 = (bf16[256,1024]{1,0:T(8,128)(2,1)S(1)}, bf16[256,1024]{1,0:T(8,128)(2,1)S(1)}, u32[]{:S(2)}, u32[]{:S(2)}) collective-permute-start(bf16[256,1024]{1,0:T(8,128)(2,1)S(1)} %collective-permute-done.12.refs_5_), channel_id=1, source_target_pairs={{1,0},{0,1},{3,2},{2,3},{5,4},{4,5},{7,6},{6,7},{9,8},{8,9},{11,10... | collective-permute-start | bytes 1572872 | tf_op jit(solution)/shard_map/ppermute | solution.py:386
  35.1 16.9 %collective-permute-start.20 = (bf16[256,512]{1,0:T(8,128)(2,1)S(1)}, bf16[256,512]{1,0:T(8,128)(2,1)S(1)}, u32[]{:S(2)}, u32[]{:S(2)}) collective-permute-start(bf16[256,512]{1,0:T(8,128)(2,1)S(1)} %collective-permute-done.15.refs_4_), channel_id=1, source_target_pairs={{0,8},{8,16},{16,24},{24,28},{28,20},{20,12},{12,4},{4,0},{1,9},{9... | collective-permute-start | bytes 786440 | tf_op jit(solution)/shard_map/ppermute | solution.py:378
  36.8 15.7 %collective-permute-start.21 = (bf16[256,512]{1,0:T(8,128)(2,1)S(1)}, bf16[256,512]{1,0:T(8,128)(2,1)S(1)}, u32[]{:S(2)}, u32[]{:S(2)}) collective-permute-start(bf16[256,512]{1,0:T(8,128)(2,1)S(1)} %collective-permute-done.16.refs_5_), channel_id=1, source_target_pairs={{8,0},{16,8},{24,16},{28,24},{20,28},{12,20},{4,12},{0,4},{9,1},{1... | collective-permute-start | bytes 786440 | tf_op jit(solution)/shard_map/ppermute | solution.py:379
  52.5 8.3 %collective-permute-start.22 = (bf16[256,512]{1,0:T(8,128)(2,1)S(1)}, bf16[256,512]{1,0:T(8,128)(2,1)S(1)}, u32[]{:S(2)}, u32[]{:S(2)}) collective-permute-start(bf16[256,512]{1,0:T(8,128)(2,1)S(1)} %collective-permute-done.20.refs_3_), channel_id=1, source_target_pairs={{0,8},{8,16},{16,24},{24,28},{28,20},{20,12},{12,4},{4,0},{1,9},{9... | collective-permute-start | bytes 786440 | tf_op jit(solution)/shard_map/ppermute | solution.py:378
  54.6 8.4 %collective-permute-start.18 = (bf16[256,256]{1,0:T(8,128)(2,1)S(1)}, bf16[256,256]{1,0:T(8,128)(2,1)S(1)}, u32[]{:S(2)}, u32[]{:S(2)}) collective-permute-start(bf16[256,256]{1,0:T(8,128)(2,1)S(1)} %shard_map.131.refs_0_), channel_id=1, source_target_pairs={{1,0},{0,1},{3,2},{2,3},{5,4},{4,5},{7,6},{6,7},{9,8},{8,9},{11,10... | collective-permute-start | bytes 393224 | tf_op jit(solution)/shard_map/ppermute | solution.py:386
  60.8 13.5 %collective-permute-start.23 = (bf16[128,512]{1,0:T(8,128)(2,1)S(1)}, bf16[128,512]{1,0:T(8,128)(2,1)S(1)}, u32[]{:S(2)}, u32[]{:S(2)}) collective-permute-start(bf16[128,512]{1,0:T(8,128)(2,1)S(1)} %slice.32), channel_id=1, source_target_pairs={{0,8},{8,16},{16,24},{24,28},{28,20},{20,12},{12,4},{4,0},{1,9},{9... | collective-permute-start | bytes 393224 | tf_op jit(solution)/shard_map/ppermute | solution.py:374
  61.2 13.5 %collective-permute-start.25 = (bf16[128,512]{1,0:T(8,128)(2,1)S(1)}, bf16[128,512]{1,0:T(8,128)(2,1)S(1)}, u32[]{:S(2)}, u32[]{:S(2)}) collective-permute-start(bf16[128,512]{1,0:T(8,128)(2,1)S(1)} %slice.33), channel_id=1, source_target_pairs={{8,0},{16,8},{24,16},{28,24},{20,28},{12,20},{4,12},{0,4},{9,1},{1... | collective-permute-start | bytes 393224 | tf_op jit(solution)/shard_map/ppermute | solution.py:375
  64.1 7.1 %collective-permute-start.26 = (bf16[272,128]{1,0:T(8,128)(2,1)S(1)}, bf16[272,128]{1,0:T(8,128)(2,1)S(1)}, u32[]{:S(2)}, u32[]{:S(2)}) collective-permute-start(bf16[272,128]{1,0:T(8,128)(2,1)S(1)} %get-tuple-element.84), channel_id=1, source_target_pairs={{0,4},{4,8},{8,12},{12,16},{16,20},{20,24},{24,28},{28,0},{1,5},{5... | collective-permute-start | bytes 208904 | tf_op jit(solution)/shard_map/ppermute | solution.py:395
  64.2 7.0 %collective-permute-start.27 = (bf16[272,128]{1,0:T(8,128)(2,1)S(1)}, bf16[272,128]{1,0:T(8,128)(2,1)S(1)}, u32[]{:S(2)}, u32[]{:S(2)}) collective-permute-start(bf16[272,128]{1,0:T(8,128)(2,1)S(1)} %get-tuple-element.85), channel_id=1, source_target_pairs={{0,8},{4,12},{8,16},{12,20},{16,24},{20,28},{24,0},{28,4},{1,9},{5... | collective-permute-start | bytes 208904 | tf_op jit(solution)/shard_map/ppermute | solution.py:395
  65.1 13.1 %collective-permute-start.28 = (bf16[272,128]{1,0:T(8,128)(2,1)S(1)}, bf16[272,128]{1,0:T(8,128)(2,1)S(1)}, u32[]{:S(2)}, u32[]{:S(2)}) collective-permute-start(bf16[272,128]{1,0:T(8,128)(2,1)S(1)} %get-tuple-element.86), channel_id=1, source_target_pairs={{0,12},{4,16},{8,20},{12,24},{16,28},{20,0},{24,4},{28,8},{1,13},{... | collective-permute-start | bytes 208904 | tf_op jit(solution)/shard_map/ppermute | solution.py:395
  80.2 9.0 %collective-permute-start.33 = (bf16[256,128]{1,0:T(8,128)(2,1)S(1)}, bf16[256,128]{1,0:T(8,128)(2,1)S(1)}, u32[]{:S(2)}, u32[]{:S(2)}) collective-permute-start(bf16[256,128]{1,0:T(8,128)(2,1)S(1)} %get-tuple-element.91.refs_0_), channel_id=1, source_target_pairs={{8,0},{12,4},{0,8},{4,12},{24,16},{28,20},{16,24},{20,28},{9,1},{1... | collective-permute-start | bytes 196616 | tf_op jit(solution)/shard_map/ppermute | solution.py:386
  81.9 7.3 %collective-permute-start.34 = (bf16[256,128]{1,0:T(8,128)(2,1)S(1)}, bf16[256,128]{1,0:T(8,128)(2,1)S(1)}, u32[]{:S(2)}, u32[]{:S(2)}) collective-permute-start(bf16[256,128]{1,0:T(8,128)(2,1)S(1)} %get-tuple-element.91.refs_0_), channel_id=1, source_target_pairs={{16,0},{20,4},{24,8},{28,12},{0,16},{4,20},{8,24},{12,28},{17,1},{... | collective-permute-start | bytes 196616 | tf_op jit(solution)/shard_map/ppermute | solution.py:386
  82.8 8.4 %collective-permute-start.35 = (bf16[256,128]{1,0:T(8,128)(2,1)S(1)}, bf16[256,128]{1,0:T(8,128)(2,1)S(1)}, u32[]{:S(2)}, u32[]{:S(2)}) collective-permute-start(bf16[256,128]{1,0:T(8,128)(2,1)S(1)} %get-tuple-element.91.refs_0_), channel_id=1, source_target_pairs={{24,0},{28,4},{16,8},{20,12},{8,16},{12,20},{0,24},{4,28},{25,1},{... | collective-permute-start | bytes 196616 | tf_op jit(solution)/shard_map/ppermute | solution.py:386
  86.1 11.7 %collective-permute-start.36 = (bf16[256,128]{1,0:T(8,128)(2,1)S(1)}, bf16[256,128]{1,0:T(8,128)(2,1)S(1)}, u32[]{:S(2)}, u32[]{:S(2)}) collective-permute-start(bf16[256,128]{1,0:T(8,128)(2,1)S(1)} %get-tuple-element.91.refs_0_), channel_id=1, source_target_pairs={{4,0},{0,4},{12,8},{8,12},{20,16},{16,20},{28,24},{24,28},{5,1},{1... | collective-permute-start | bytes 196616 | tf_op jit(solution)/shard_map/ppermute | solution.py:386
  89.1 8.7 %collective-permute-start.37 = (bf16[256,128]{1,0:T(8,128)(2,1)S(1)}, bf16[256,128]{1,0:T(8,128)(2,1)S(1)}, u32[]{:S(2)}, u32[]{:S(2)}) collective-permute-start(bf16[256,128]{1,0:T(8,128)(2,1)S(1)} %collective-permute-done.33.refs_1_), channel_id=1, source_target_pairs={{4,0},{0,4},{12,8},{8,12},{20,16},{16,20},{28,24},{24,28},{5,1},{1... | collective-permute-start | bytes 196616 | tf_op jit(solution)/shard_map/ppermute | solution.py:386
  89.2 8.6 %collective-permute-start.38 = (bf16[256,128]{1,0:T(8,128)(2,1)S(1)}, bf16[256,128]{1,0:T(8,128)(2,1)S(1)}, u32[]{:S(2)}, u32[]{:S(2)}) collective-permute-start(bf16[256,128]{1,0:T(8,128)(2,1)S(1)} %collective-permute-done.34.refs_2_), channel_id=1, source_target_pairs={{4,0},{0,4},{12,8},{8,12},{20,16},{16,20},{28,24},{24,28},{5,1},{1... | collective-permute-start | bytes 196616 | tf_op jit(solution)/shard_map/ppermute | solution.py:386
  (21 other events, 123.9 us)

commit v4 on v3

--- a/solution.py
+++ b/solution.py
@@ -45,14 +45,12 @@
     d_hidden = -mm(values, w_two_t)
     sig = jax.nn.sigmoid(gate)
     silu = gate * sig
-    d_gate = d_hidden * up * sig * (1.0 + gate * (1.0 - sig))
+    d_gate = d_hidden * up * (sig + silu * (1.0 - sig))
     d_up = d_hidden * silu
     hidden = silu * up
-    return (
-        mm_tn(keys, d_gate.astype(BF16)),
-        mm_tn(keys, d_up.astype(BF16)),
-        -mm_tn(values, hidden.astype(BF16)),
-    )
+    both = mm_tn(keys, jnp.concatenate([d_gate.astype(BF16), d_up.astype(BF16)], axis=1))
+    width = d_gate.shape[1]
+    return (both[:, :width], both[:, width:], -mm_tn(values, hidden.astype(BF16)))
 
 
 def orthogonalize(mats):

time: 99.1 us -> 98.9 us (level)
  transfers between devices with their start and end apart: 40 -> 40, of which waited for: 13 -> 14; matrix products, arithmetic and copies ran while one was open for 2% -> 2% of each run, Pallas kernels for 27% -> 27%
where the time goes in v4:
time: 98.9 us; the launch traced here: 98.7 us
  starting transfers between devices  40.3 us (41%)
  Pallas kernels  28.1 us (28%)
  waiting for transfers between devices  26.2 us (26%)
  local copies, waits for them, and re-layouts  2.43 us (2%)
    pallas_call x14, Pallas kernels, call(): pl.pallas_call(kernel, out_shape=tuple((jax.ShapeDtypeStruct(o.shape, o.d...  28.1 us
    ppermute x16, starting transfers between devices, partner(): return lax.ppermute(block, axis, [(i ^ bit, i) for i in range(size)])  14.7 us
    ppermute x6, waiting for transfers between devices, step(): self.up = lax.ppermute(up, self.axis, self.ahead)  13.9 us
    ppermute x6, starting transfers between devices, step(): self.up = lax.ppermute(up, self.axis, self.ahead)  9.51 us
    ppermute x7, starting transfers between devices, shifted(): got[shift - 1] = lax.ppermute(blocks[shift - 1], axis, pairs)  9.41 us
    ppermute x16, waiting for transfers between devices, partner(): return lax.ppermute(block, axis, [(i ^ bit, i) for i in range(size)])  3.94 us
    ppermute x7, waiting for transfers between devices, shifted(): got[shift - 1] = lax.ppermute(blocks[shift - 1], axis, pairs)  3.63 us
    ppermute x1, waiting for transfers between devices, from_behind(): return lax.ppermute(block, axis, [((i - 1) % size, i) for i in range(size)])  2.62 us
  transfers between devices with their start and end apart: 40, of which 14 were waited for; matrix products, arithmetic and copies ran while one was open for 2% of the time, Pallas kernels for 27%

profile of v4, /device:TPU:0, one launch (start us, length us, event | category | flops | bytes accessed | tf_op | source)
XLA Modules:
  0.0 98.7 jit_solution(17426043992572038185)
XLA Ops:
  1.9 3.1 %collective-permute-start = (bf16[256,512]{1,0:T(8,128)(2,1)S(1)}, bf16[256,512]{1,0:T(8,128)(2,1)S(1)}, u32[]{:S(2)}, u32[]{:S(2)}) collective-permute-start(bf16[256,512]{1,0:T(8,128)(2,1)S(1)} %get-tuple-element.72.refs_3_.own_ref), channel_id=1, source_target_pairs={{0,8},{8,16},{16,24},{24,28},{28,20},{20,12},{12,4},{4,0},{1,9},{9... | collective-permute-start | bytes 786440 | tf_op jit(solution)/shard_map/ppermute | solution.py:376
  5.0 6.2 %collective-permute-done.refs_4_.refs_0_ = bf16[256,512]{1,0:T(8,128)(2,1)S(1)} collective-permute-done((bf16[256,512]{1,0:T(8,128)(2,1)S(1)}, bf16[256,512]{1,0:T(8,128)(2,1)S(1)}, u32[]{:S(2)}, u32[]{:S(2)}) %collective-permute-start) | collective-permute-done | bytes 262176 | tf_op jit(solution)/shard_map/ppermute | solution.py:376
  11.2 1.8 %collective-permute-start.1 = (bf16[256,512]{1,0:T(8,128)(2,1)S(1)}, bf16[256,512]{1,0:T(8,128)(2,1)S(1)}, u32[]{:S(2)}, u32[]{:S(2)}) collective-permute-start(bf16[256,512]{1,0:T(8,128)(2,1)S(1)} %collective-permute-done.refs_4_.refs_0_), channel_id=1, source_target_pairs={{0,8},{8,16},{16,24},{24,28},{28,20},{20,12},{12,4},{4,0},{1,9},{9... | collective-permute-start | bytes 786440 | tf_op jit(solution)/shard_map/ppermute | solution.py:376
  14.5 2.1 %shard_map.127 = (f32[256,512]{1,0:T(8,128)S(1)}, f32[256,512]{1,0:T(8,128)S(1)}, f32[256,512]{1,0:T(8,128)S(1)}) custom-call(f32[256,512]{1,0:T(8,128)S(1)} %bitcast.21, f32[256,512]{1,0:T(8,128)S(1)} %bitcast.26, f32[256,512]{1,0:T(8,128)S(1)} %bitcast.16, bf16[256,512]{1,0:T(8,128)(2,1)S(1)} %get-tuple-element.72.refs_3_.own_ref, ...), custom_call_target="tpu_custom_call" | custom-call | flops 1207959552 | bytes 3932160 | tf_op jit(solution)/shard_map/pallas_call | solution.py:121
  16.6 2.1 %collective-permute-done.1.refs_3_.refs_2_ = bf16[256,512]{1,0:T(8,128)(2,1)S(1)} collective-permute-done((bf16[256,512]{1,0:T(8,128)(2,1)S(1)}, bf16[256,512]{1,0:T(8,128)(2,1)S(1)}, u32[]{:S(2)}, u32[]{:S(2)}) %collective-permute-start.1) | collective-permute-done | bytes 262176 | tf_op jit(solution)/shard_map/ppermute | solution.py:376
  22.1 3.1 %collective-permute-done.3.refs_3_.refs_4_ = bf16[256,512]{1,0:T(8,128)(2,1)S(1)} collective-permute-done((bf16[256,512]{1,0:T(8,128)(2,1)S(1)}, bf16[256,512]{1,0:T(8,128)(2,1)S(1)}, u32[]{:S(2)}, u32[]{:S(2)}) %collective-permute-start.3) | collective-permute-done | bytes 262176 | tf_op jit(solution)/shard_map/ppermute | solution.py:376
  30.0 1.6 %collective-permute-start.7 = (bf16[128,512]{1,0:T(8,128)(2,1)S(1)}, bf16[128,512]{1,0:T(8,128)(2,1)S(1)}, u32[]{:S(2)}, u32[]{:S(2)}) collective-permute-start(bf16[128,512]{1,0:T(8,128)(2,1)S(1)} %slice.28), channel_id=1, source_target_pairs={{0,8},{8,16},{16,24},{24,28},{28,20},{20,12},{12,4},{4,0},{1,9},{9... | collective-permute-start | bytes 393224 | tf_op jit(solution)/shard_map/ppermute | solution.py:372
  35.0 1.6 %collective-permute-start.20 = (bf16[256,512]{1,0:T(8,128)(2,1)S(1)}, bf16[256,512]{1,0:T(8,128)(2,1)S(1)}, u32[]{:S(2)}, u32[]{:S(2)}) collective-permute-start(bf16[256,512]{1,0:T(8,128)(2,1)S(1)} %collective-permute-done.15.refs_4_), channel_id=1, source_target_pairs={{0,8},{8,16},{16,24},{24,28},{28,20},{20,12},{12,4},{4,0},{1,9},{9... | collective-permute-start | bytes 786440 | tf_op jit(solution)/shard_map/ppermute | solution.py:376
  37.2 5.8 %shard_map.130 = (f32[256,512]{1,0:T(8,128)S(1)}, f32[256,512]{1,0:T(8,128)S(1)}, f32[256,512]{1,0:T(8,128)S(1)}, f32[256,256]{1,0:T(8,128)S(1)}) custom-call(f32[256,512]{1,0:T(8,128)S(1)} %bitcast.24, f32[256,512]{1,0:T(8,128)S(1)} %bitcast.29, f32[256,512]{1,0:T(8,128)S(1)} %bitcast.19, f32[256,512]{1,0:T(8,128)S(1)} %get-tuple-element.66.refs_3_, ...), custom_call_target="tpu_custom_call" | custom-call | flops 5033164800 | bytes 5505024 | tf_op jit(solution)/shard_map/pallas_call | solution.py:121
  43.0 2.6 %collective-permute-done.6.behind_ref = bf16[256,512]{1,0:T(8,128)(2,1)S(1)} collective-permute-done((bf16[256,512]{1,0:T(8,128)(2,1)S(1)}, bf16[256,512]{1,0:T(8,128)(2,1)S(1)}, u32[]{:S(2)}, u32[]{:S(2)}) %collective-permute-start.6) | collective-permute-done | bytes 262176 | tf_op jit(solution)/shard_map/ppermute | solution.py:408
  49.9 1.9 %collective-permute-done.17.refs_1_ = bf16[256,256]{1,0:T(8,128)(2,1)S(1)} collective-permute-done((bf16[256,256]{1,0:T(8,128)(2,1)S(1)}, bf16[256,256]{1,0:T(8,128)(2,1)S(1)}, u32[]{:S(2)}, u32[]{:S(2)}) %collective-permute-start.17) | collective-permute-done | bytes 131104 | tf_op jit(solution)/shard_map/ppermute | solution.py:384
  52.3 2.0 %collective-permute-done.9.refs_1_ = bf16[256,256]{1,0:T(8,128)(2,1)S(1)} collective-permute-done((bf16[256,256]{1,0:T(8,128)(2,1)S(1)}, bf16[256,256]{1,0:T(8,128)(2,1)S(1)}, u32[]{:S(2)}, u32[]{:S(2)}) %collective-permute-start.9) | collective-permute-done | bytes 131104 | tf_op jit(solution)/shard_map/ppermute | solution.py:384
  54.9 2.1 %shard_map.137 = (f32[256,512]{1,0:T(8,128)S(1)}, f32[256,512]{1,0:T(8,128)S(1)}, f32[256,512]{1,0:T(8,128)S(1)}) custom-call(f32[256,512]{1,0:T(8,128)S(1)} %get-tuple-element.92.refs_0_, f32[256,512]{1,0:T(8,128)S(1)} %get-tuple-element.93.refs_1_, f32[256,512]{1,0:T(8,128)S(1)} %get-tuple-element.94.refs_2_, ...), custom_call_target="tpu_custom_call" | custom-call | flops 1207959552 | bytes 3932160 | tf_op jit(solution)/shard_map/pallas_call | solution.py:121
  58.2 2.4 %collective-permute-done.22.refs_3_ = bf16[256,512]{1,0:T(8,128)(2,1)S(1)} collective-permute-done((bf16[256,512]{1,0:T(8,128)(2,1)S(1)}, bf16[256,512]{1,0:T(8,128)(2,1)S(1)}, u32[]{:S(2)}, u32[]{:S(2)}) %collective-permute-start.22) | collective-permute-done | bytes 262176 | tf_op jit(solution)/shard_map/ppermute | solution.py:376
  61.0 1.8 %collective-permute-start.25 = (bf16[128,512]{1,0:T(8,128)(2,1)S(1)}, bf16[128,512]{1,0:T(8,128)(2,1)S(1)}, u32[]{:S(2)}, u32[]{:S(2)}) collective-permute-start(bf16[128,512]{1,0:T(8,128)(2,1)S(1)} %slice.33), channel_id=1, source_target_pairs={{8,0},{16,8},{24,16},{28,24},{20,28},{12,20},{4,12},{0,4},{9,1},{1... | collective-permute-start | bytes 393224 | tf_op jit(solution)/shard_map/ppermute | solution.py:373
  64.8 3.2 %collective-permute-start.28 = (bf16[272,128]{1,0:T(8,128)(2,1)S(1)}, bf16[272,128]{1,0:T(8,128)(2,1)S(1)}, u32[]{:S(2)}, u32[]{:S(2)}) collective-permute-start(bf16[272,128]{1,0:T(8,128)(2,1)S(1)} %get-tuple-element.86), channel_id=1, source_target_pairs={{0,12},{4,16},{8,20},{12,24},{16,28},{20,0},{24,4},{28,8},{1,13},{... | collective-permute-start | bytes 208904 | tf_op jit(solution)/shard_map/ppermute | solution.py:393
  68.8 2.3 %collective-permute-done.26.rest_0_ = bf16[272,128]{1,0:T(8,128)(2,1)S(1)} collective-permute-done((bf16[272,128]{1,0:T(8,128)(2,1)S(1)}, bf16[272,128]{1,0:T(8,128)(2,1)S(1)}, u32[]{:S(2)}, u32[]{:S(2)}) %collective-permute-start.26) | collective-permute-done | bytes 69664 | tf_op jit(solution)/shard_map/ppermute | solution.py:393
  71.0 3.0 %collective-permute-start.30 = (bf16[272,128]{1,0:T(8,128)(2,1)S(1)}, bf16[272,128]{1,0:T(8,128)(2,1)S(1)}, u32[]{:S(2)}, u32[]{:S(2)}) collective-permute-start(bf16[272,128]{1,0:T(8,128)(2,1)S(1)} %get-tuple-element.88), channel_id=1, source_target_pairs={{0,20},{4,24},{8,28},{12,0},{16,4},{20,8},{24,12},{28,16},{1,21},{... | collective-permute-start | bytes 208904 | tf_op jit(solution)/shard_map/ppermute | solution.py:393
  74.4 2.0 %collective-permute-start.32 = (bf16[272,128]{1,0:T(8,128)(2,1)S(1)}, bf16[272,128]{1,0:T(8,128)(2,1)S(1)}, u32[]{:S(2)}, u32[]{:S(2)}) collective-permute-start(bf16[272,128]{1,0:T(8,128)(2,1)S(1)} %get-tuple-element.90), channel_id=1, source_target_pairs={{0,28},{4,0},{8,4},{12,8},{16,12},{20,16},{24,20},{28,24},{1,29},{... | collective-permute-start | bytes 208904 | tf_op jit(solution)/shard_map/ppermute | solution.py:393
  80.0 1.7 %collective-permute-start.33 = (bf16[256,128]{1,0:T(8,128)(2,1)S(1)}, bf16[256,128]{1,0:T(8,128)(2,1)S(1)}, u32[]{:S(2)}, u32[]{:S(2)}) collective-permute-start(bf16[256,128]{1,0:T(8,128)(2,1)S(1)} %get-tuple-element.91.refs_0_), channel_id=1, source_target_pairs={{8,0},{12,4},{0,8},{4,12},{24,16},{28,20},{16,24},{20,28},{9,1},{1... | collective-permute-start | bytes 196616 | tf_op jit(solution)/shard_map/ppermute | solution.py:384
  82.6 1.9 %collective-permute-start.35 = (bf16[256,128]{1,0:T(8,128)(2,1)S(1)}, bf16[256,128]{1,0:T(8,128)(2,1)S(1)}, u32[]{:S(2)}, u32[]{:S(2)}) collective-permute-start(bf16[256,128]{1,0:T(8,128)(2,1)S(1)} %get-tuple-element.91.refs_0_), channel_id=1, source_target_pairs={{24,0},{28,4},{16,8},{20,12},{8,16},{12,20},{0,24},{4,28},{25,1},{... | collective-permute-start | bytes 196616 | tf_op jit(solution)/shard_map/ppermute | solution.py:384
  85.9 3.0 %collective-permute-start.36 = (bf16[256,128]{1,0:T(8,128)(2,1)S(1)}, bf16[256,128]{1,0:T(8,128)(2,1)S(1)}, u32[]{:S(2)}, u32[]{:S(2)}) collective-permute-start(bf16[256,128]{1,0:T(8,128)(2,1)S(1)} %get-tuple-element.91.refs_0_), channel_id=1, source_target_pairs={{4,0},{0,4},{12,8},{8,12},{20,16},{16,20},{28,24},{24,28},{5,1},{1... | collective-permute-start | bytes 196616 | tf_op jit(solution)/shard_map/ppermute | solution.py:384
  88.9 1.9 %collective-permute-start.38 = (bf16[256,128]{1,0:T(8,128)(2,1)S(1)}, bf16[256,128]{1,0:T(8,128)(2,1)S(1)}, u32[]{:S(2)}, u32[]{:S(2)}) collective-permute-start(bf16[256,128]{1,0:T(8,128)(2,1)S(1)} %collective-permute-done.34.refs_2_), channel_id=1, source_target_pairs={{4,0},{0,4},{12,8},{8,12},{20,16},{16,20},{28,24},{24,28},{5,1},{1... | collective-permute-start | bytes 196616 | tf_op jit(solution)/shard_map/ppermute | solution.py:384
  91.4 6.2 %shard_map.140 = (f32[1,256,512]{2,1,0:T(8,128)}, f32[1,256,512]{2,1,0:T(8,128)}, f32[1,512,256]{2,1,0:T(8,128)}) custom-call(f32[256,512]{1,0:T(8,128)S(1)} %get-tuple-element.92.refs_0_, f32[256,512]{1,0:T(8,128)S(1)} %get-tuple-element.93.refs_1_, f32[256,512]{1,0:T(8,128)S(1)} %get-tuple-element.94.refs_2_, f32[256,512]{1,0:T(8,128)S(1)} %get-tuple-element.101.refs_3_, ...), custom_call_target="tpu_custom_call" | custom-call | flops 5033164800 | bytes 4980736 | tf_op jit(solution)/shard_map/pallas_call | solution.py:121
  (88 shorter events, 32.3 us)
Async XLA Ops:
  1.9 9.3 %collective-permute-start = (bf16[256,512]{1,0:T(8,128)(2,1)S(1)}, bf16[256,512]{1,0:T(8,128)(2,1)S(1)}, u32[]{:S(2)}, u32[]{:S(2)}) collective-permute-start(bf16[256,512]{1,0:T(8,128)(2,1)S(1)} %get-tuple-element.72.refs_3_.own_ref), channel_id=1, source_target_pairs={{0,8},{8,16},{16,24},{24,28},{28,20},{20,12},{12,4},{4,0},{1,9},{9... | collective-permute-start | bytes 786440 | tf_op jit(solution)/shard_map/ppermute | solution.py:376
  5.0 8.0 %collective-permute-start.2 = (bf16[256,512]{1,0:T(8,128)(2,1)S(1)}, bf16[256,512]{1,0:T(8,128)(2,1)S(1)}, u32[]{:S(2)}, u32[]{:S(2)}) collective-permute-start(bf16[256,512]{1,0:T(8,128)(2,1)S(1)} %get-tuple-element.72.refs_3_.own_ref), channel_id=1, source_target_pairs={{8,0},{16,8},{24,16},{28,24},{20,28},{12,20},{4,12},{0,4},{9,1},{1... | collective-permute-start | bytes 786440 | tf_op jit(solution)/shard_map/ppermute | solution.py:377
  11.2 7.5 %collective-permute-start.1 = (bf16[256,512]{1,0:T(8,128)(2,1)S(1)}, bf16[256,512]{1,0:T(8,128)(2,1)S(1)}, u32[]{:S(2)}, u32[]{:S(2)}) collective-permute-start(bf16[256,512]{1,0:T(8,128)(2,1)S(1)} %collective-permute-done.refs_4_.refs_0_), channel_id=1, source_target_pairs={{0,8},{8,16},{16,24},{24,28},{28,20},{20,12},{12,4},{4,0},{1,9},{9... | collective-permute-start | bytes 786440 | tf_op jit(solution)/shard_map/ppermute | solution.py:376
  13.0 7.2 %collective-permute-start.4 = (bf16[256,512]{1,0:T(8,128)(2,1)S(1)}, bf16[256,512]{1,0:T(8,128)(2,1)S(1)}, u32[]{:S(2)}, u32[]{:S(2)}) collective-permute-start(bf16[256,512]{1,0:T(8,128)(2,1)S(1)} %collective-permute-done.2.refs_5_.refs_1_), channel_id=1, source_target_pairs={{8,0},{16,8},{24,16},{28,24},{20,28},{12,20},{4,12},{0,4},{9,1},{1... | collective-permute-start | bytes 786440 | tf_op jit(solution)/shard_map/ppermute | solution.py:377
  20.7 12.9 %collective-permute-start.12 = (bf16[256,1024]{1,0:T(8,128)(2,1)S(1)}, bf16[256,1024]{1,0:T(8,128)(2,1)S(1)}, u32[]{:S(2)}, u32[]{:S(2)}) collective-permute-start(bf16[256,1024]{1,0:T(8,128)(2,1)S(1)} %copy-done.3), channel_id=1, source_target_pairs={{2,0},{3,1},{0,2},{1,3},{6,4},{7,5},{4,6},{5,7},{10,8},{11,9},{8,1... | collective-permute-start | bytes 1572872 | tf_op jit(solution)/shard_map/ppermute | solution.py:384
  26.6 7.0 %collective-permute-start.15 = (bf16[256,512]{1,0:T(8,128)(2,1)S(1)}, bf16[256,512]{1,0:T(8,128)(2,1)S(1)}, u32[]{:S(2)}, u32[]{:S(2)}) collective-permute-start(bf16[256,512]{1,0:T(8,128)(2,1)S(1)} %get-tuple-element.75.own_ref.refs_3_), channel_id=1, source_target_pairs={{0,8},{8,16},{16,24},{24,28},{28,20},{20,12},{12,4},{4,0},{1,9},{9... | collective-permute-start | bytes 786440 | tf_op jit(solution)/shard_map/ppermute | solution.py:376
  33.6 15.7 %collective-permute-start.13 = (bf16[256,1024]{1,0:T(8,128)(2,1)S(1)}, bf16[256,1024]{1,0:T(8,128)(2,1)S(1)}, u32[]{:S(2)}, u32[]{:S(2)}) collective-permute-start(bf16[256,1024]{1,0:T(8,128)(2,1)S(1)} %copy-done.3), channel_id=1, source_target_pairs={{1,0},{0,1},{3,2},{2,3},{5,4},{4,5},{7,6},{6,7},{9,8},{8,9},{11,10... | collective-permute-start | bytes 1572872 | tf_op jit(solution)/shard_map/ppermute | solution.py:384
  33.7 11.9 %collective-permute-start.6 = (bf16[256,512]{1,0:T(8,128)(2,1)S(1)}, bf16[256,512]{1,0:T(8,128)(2,1)S(1)}, u32[]{:S(2)}, u32[]{:S(2)}) collective-permute-start(bf16[256,512]{1,0:T(8,128)(2,1)S(1)} %get-tuple-element.60), channel_id=1, source_target_pairs={{28,0},{0,4},{4,8},{8,12},{12,16},{16,20},{20,24},{24,28},{29,1},{... | collective-permute-start | bytes 786440 | tf_op jit(solution)/shard_map/ppermute | solution.py:408
  34.6 22.4 %collective-permute-start.14 = (bf16[256,1024]{1,0:T(8,128)(2,1)S(1)}, bf16[256,1024]{1,0:T(8,128)(2,1)S(1)}, u32[]{:S(2)}, u32[]{:S(2)}) collective-permute-start(bf16[256,1024]{1,0:T(8,128)(2,1)S(1)} %collective-permute-done.12.refs_5_), channel_id=1, source_target_pairs={{1,0},{0,1},{3,2},{2,3},{5,4},{4,5},{7,6},{6,7},{9,8},{8,9},{11,10... | collective-permute-start | bytes 1572872 | tf_op jit(solution)/shard_map/ppermute | solution.py:384
  35.0 16.8 %collective-permute-start.20 = (bf16[256,512]{1,0:T(8,128)(2,1)S(1)}, bf16[256,512]{1,0:T(8,128)(2,1)S(1)}, u32[]{:S(2)}, u32[]{:S(2)}) collective-permute-start(bf16[256,512]{1,0:T(8,128)(2,1)S(1)} %collective-permute-done.15.refs_4_), channel_id=1, source_target_pairs={{0,8},{8,16},{16,24},{24,28},{28,20},{20,12},{12,4},{4,0},{1,9},{9... | collective-permute-start | bytes 786440 | tf_op jit(solution)/shard_map/ppermute | solution.py:376
  36.7 15.6 %collective-permute-start.21 = (bf16[256,512]{1,0:T(8,128)(2,1)S(1)}, bf16[256,512]{1,0:T(8,128)(2,1)S(1)}, u32[]{:S(2)}, u32[]{:S(2)}) collective-permute-start(bf16[256,512]{1,0:T(8,128)(2,1)S(1)} %collective-permute-done.16.refs_5_), channel_id=1, source_target_pairs={{8,0},{16,8},{24,16},{28,24},{20,28},{12,20},{4,12},{0,4},{9,1},{1... | collective-permute-start | bytes 786440 | tf_op jit(solution)/shard_map/ppermute | solution.py:377
  52.3 8.3 %collective-permute-start.22 = (bf16[256,512]{1,0:T(8,128)(2,1)S(1)}, bf16[256,512]{1,0:T(8,128)(2,1)S(1)}, u32[]{:S(2)}, u32[]{:S(2)}) collective-permute-start(bf16[256,512]{1,0:T(8,128)(2,1)S(1)} %collective-permute-done.20.refs_3_), channel_id=1, source_target_pairs={{0,8},{8,16},{16,24},{24,28},{28,20},{20,12},{12,4},{4,0},{1,9},{9... | collective-permute-start | bytes 786440 | tf_op jit(solution)/shard_map/ppermute | solution.py:376
  54.4 8.4 %collective-permute-start.18 = (bf16[256,256]{1,0:T(8,128)(2,1)S(1)}, bf16[256,256]{1,0:T(8,128)(2,1)S(1)}, u32[]{:S(2)}, u32[]{:S(2)}) collective-permute-start(bf16[256,256]{1,0:T(8,128)(2,1)S(1)} %shard_map.131.refs_0_), channel_id=1, source_target_pairs={{1,0},{0,1},{3,2},{2,3},{5,4},{4,5},{7,6},{6,7},{9,8},{8,9},{11,10... | collective-permute-start | bytes 393224 | tf_op jit(solution)/shard_map/ppermute | solution.py:384
  60.6 13.5 %collective-permute-start.23 = (bf16[128,512]{1,0:T(8,128)(2,1)S(1)}, bf16[128,512]{1,0:T(8,128)(2,1)S(1)}, u32[]{:S(2)}, u32[]{:S(2)}) collective-permute-start(bf16[128,512]{1,0:T(8,128)(2,1)S(1)} %slice.32), channel_id=1, source_target_pairs={{0,8},{8,16},{16,24},{24,28},{28,20},{20,12},{12,4},{4,0},{1,9},{9... | collective-permute-start | bytes 393224 | tf_op jit(solution)/shard_map/ppermute | solution.py:372
  61.0 13.4 %collective-permute-start.25 = (bf16[128,512]{1,0:T(8,128)(2,1)S(1)}, bf16[128,512]{1,0:T(8,128)(2,1)S(1)}, u32[]{:S(2)}, u32[]{:S(2)}) collective-permute-start(bf16[128,512]{1,0:T(8,128)(2,1)S(1)} %slice.33), channel_id=1, source_target_pairs={{8,0},{16,8},{24,16},{28,24},{20,28},{12,20},{4,12},{0,4},{9,1},{1... | collective-permute-start | bytes 393224 | tf_op jit(solution)/shard_map/ppermute | solution.py:373
  64.0 7.1 %collective-permute-start.26 = (bf16[272,128]{1,0:T(8,128)(2,1)S(1)}, bf16[272,128]{1,0:T(8,128)(2,1)S(1)}, u32[]{:S(2)}, u32[]{:S(2)}) collective-permute-start(bf16[272,128]{1,0:T(8,128)(2,1)S(1)} %get-tuple-element.84), channel_id=1, source_target_pairs={{0,4},{4,8},{8,12},{12,16},{16,20},{20,24},{24,28},{28,0},{1,5},{5... | collective-permute-start | bytes 208904 | tf_op jit(solution)/shard_map/ppermute | solution.py:393
  64.0 7.0 %collective-permute-start.27 = (bf16[272,128]{1,0:T(8,128)(2,1)S(1)}, bf16[272,128]{1,0:T(8,128)(2,1)S(1)}, u32[]{:S(2)}, u32[]{:S(2)}) collective-permute-start(bf16[272,128]{1,0:T(8,128)(2,1)S(1)} %get-tuple-element.85), channel_id=1, source_target_pairs={{0,8},{4,12},{8,16},{12,20},{16,24},{20,28},{24,0},{28,4},{1,9},{5... | collective-permute-start | bytes 208904 | tf_op jit(solution)/shard_map/ppermute | solution.py:393
  64.8 13.0 %collective-permute-start.28 = (bf16[272,128]{1,0:T(8,128)(2,1)S(1)}, bf16[272,128]{1,0:T(8,128)(2,1)S(1)}, u32[]{:S(2)}, u32[]{:S(2)}) collective-permute-start(bf16[272,128]{1,0:T(8,128)(2,1)S(1)} %get-tuple-element.86), channel_id=1, source_target_pairs={{0,12},{4,16},{8,20},{12,24},{16,28},{20,0},{24,4},{28,8},{1,13},{... | collective-permute-start | bytes 208904 | tf_op jit(solution)/shard_map/ppermute | solution.py:393
  80.0 8.9 %collective-permute-start.33 = (bf16[256,128]{1,0:T(8,128)(2,1)S(1)}, bf16[256,128]{1,0:T(8,128)(2,1)S(1)}, u32[]{:S(2)}, u32[]{:S(2)}) collective-permute-start(bf16[256,128]{1,0:T(8,128)(2,1)S(1)} %get-tuple-element.91.refs_0_), channel_id=1, source_target_pairs={{8,0},{12,4},{0,8},{4,12},{24,16},{28,20},{16,24},{20,28},{9,1},{1... | collective-permute-start | bytes 196616 | tf_op jit(solution)/shard_map/ppermute | solution.py:384
  81.7 7.2 %collective-permute-start.34 = (bf16[256,128]{1,0:T(8,128)(2,1)S(1)}, bf16[256,128]{1,0:T(8,128)(2,1)S(1)}, u32[]{:S(2)}, u32[]{:S(2)}) collective-permute-start(bf16[256,128]{1,0:T(8,128)(2,1)S(1)} %get-tuple-element.91.refs_0_), channel_id=1, source_target_pairs={{16,0},{20,4},{24,8},{28,12},{0,16},{4,20},{8,24},{12,28},{17,1},{... | collective-permute-start | bytes 196616 | tf_op jit(solution)/shard_map/ppermute | solution.py:384
  82.6 8.3 %collective-permute-start.35 = (bf16[256,128]{1,0:T(8,128)(2,1)S(1)}, bf16[256,128]{1,0:T(8,128)(2,1)S(1)}, u32[]{:S(2)}, u32[]{:S(2)}) collective-permute-start(bf16[256,128]{1,0:T(8,128)(2,1)S(1)} %get-tuple-element.91.refs_0_), channel_id=1, source_target_pairs={{24,0},{28,4},{16,8},{20,12},{8,16},{12,20},{0,24},{4,28},{25,1},{... | collective-permute-start | bytes 196616 | tf_op jit(solution)/shard_map/ppermute | solution.py:384
  85.9 11.8 %collective-permute-start.36 = (bf16[256,128]{1,0:T(8,128)(2,1)S(1)}, bf16[256,128]{1,0:T(8,128)(2,1)S(1)}, u32[]{:S(2)}, u32[]{:S(2)}) collective-permute-start(bf16[256,128]{1,0:T(8,128)(2,1)S(1)} %get-tuple-element.91.refs_0_), channel_id=1, source_target_pairs={{4,0},{0,4},{12,8},{8,12},{20,16},{16,20},{28,24},{24,28},{5,1},{1... | collective-permute-start | bytes 196616 | tf_op jit(solution)/shard_map/ppermute | solution.py:384
  88.8 8.8 %collective-permute-start.37 = (bf16[256,128]{1,0:T(8,128)(2,1)S(1)}, bf16[256,128]{1,0:T(8,128)(2,1)S(1)}, u32[]{:S(2)}, u32[]{:S(2)}) collective-permute-start(bf16[256,128]{1,0:T(8,128)(2,1)S(1)} %collective-permute-done.33.refs_1_), channel_id=1, source_target_pairs={{4,0},{0,4},{12,8},{8,12},{20,16},{16,20},{28,24},{24,28},{5,1},{1... | collective-permute-start | bytes 196616 | tf_op jit(solution)/shard_map/ppermute | solution.py:384
  88.9 8.7 %collective-permute-start.38 = (bf16[256,128]{1,0:T(8,128)(2,1)S(1)}, bf16[256,128]{1,0:T(8,128)(2,1)S(1)}, u32[]{:S(2)}, u32[]{:S(2)}) collective-permute-start(bf16[256,128]{1,0:T(8,128)(2,1)S(1)} %collective-permute-done.34.refs_2_), channel_id=1, source_target_pairs={{4,0},{0,4},{12,8},{8,12},{20,16},{16,20},{28,24},{24,28},{5,1},{1... | collective-permute-start | bytes 196616 | tf_op jit(solution)/shard_map/ppermute | solution.py:384
  (21 other events, 123.6 us)
